TPU v7x, 256 devices: a whole 4x4x8 slice. The times are simulated.
256 devices in a mesh: section: 2 (over core), row: 8 (over z), col: 16 (over y, x).
Axes of the slice: x: 4, y: 4, z: 8, core: 2. Of those that a mesh axis runs over, the one named last changes fastest.
Arguments:
- hidden_in: bfloat16 [2, 1024, 8192], P('section', 'col', 'row'), may hold values from -80 to 80
- norm_gain: float32 [2, 8192], P('section', 'row'), may hold values from 0.1 to 1.9
- gate_saved: bfloat16 [2, 1024, 14336], P('section', 'row', 'col'), may hold values from -6 to 6
- up_saved: bfloat16 [2, 1024, 14336], P('section', 'row', 'col'), may hold values from -6 to 6
- w_gate: bfloat16 [2, 8192, 14336], P('section', 'row', 'col'), may hold values from -0.0625 to 0.0625
- w_up: bfloat16 [2, 8192, 14336], P('section', 'row', 'col'), may hold values from -0.0625 to 0.0625
- w_down: bfloat16 [2, 14336, 8192], P('section', 'col', 'row'), may hold values from -0.046875 to 0.046875
- out_grad: bfloat16 [1024, 8192], P('col', 'row'), may hold values from -6 to 6
Outputs:
- in_grad: bfloat16 [2, 1024, 8192], P('section', 'col', 'row')
- gain_grad: float32 [2, 8192], P('section', 'row')
- grad_gate: bfloat16 [2, 8192, 14336], P('section', 'row', 'col')
- grad_up: bfloat16 [2, 8192, 14336], P('section', 'row', 'col')
- grad_down: bfloat16 [2, 14336, 8192], P('section', 'col', 'row')
All inputs are finite; a program needn't handle non-finite values.
Results may differ from a plain program's by a relative error of at most 0.03.
Values may be sent and summed in bfloat16 or wider, within the bound.
No kernel may reach another device: no remote copies, remote signals or barrier semaphores. Data moves between devices by JAX's collectives and lax.ppermute only.
A program may use at most 128 MiB of HBM per device.

v0:
```python
import jax
import jax.numpy as jnp
from jax import lax
from jax.sharding import PartitionSpec as P

D = 8192
EPSILON = 1e-05

bf16 = jnp.bfloat16
f32 = jnp.float32


def dot(left, right, dims):
    return lax.dot_general(left, right, (dims, ((), ())), preferred_element_type=f32)


def swap(block):
    return lax.ppermute(block, "section", [(0, 1), (1, 0)])


def after(block, event):
    return lax.optimization_barrier((block, event))[0]


def exchange(blocks, axis):
    return lax.all_to_all(blocks, axis, 0, 0)


def spread(block, axis):
    copies = jnp.broadcast_to(block[None], (lax.axis_size(axis),) + block.shape)
    return exchange(copies, axis)


def unit_grads(hidden_grad, saved):
    grad_f = hidden_grad.astype(f32)
    gate_f, up_f = saved[0].astype(f32), saved[1].astype(f32)
    sig = jax.nn.sigmoid(gate_f)
    gate_grad = (grad_f * up_f * sig * (1.0 + gate_f * (1.0 - sig))).astype(bf16)
    up_grad = (grad_f * gate_f * sig).astype(bf16)
    return gate_grad, up_grad


def into_features(gate_grad, up_grad, gate_w, up_w):
    partial = dot(gate_grad, gate_w, ((1,), (1,))) + dot(up_grad, up_w, ((1,), (1,)))
    return partial.astype(bf16)


def body(hidden_in, norm_gain, gate_saved, up_saved, w_gate, w_up, w_down, out_grad):
    rows, cols = lax.axis_size("row"), lax.axis_size("col")
    first = lax.axis_index("section") == 0
    features = hidden_in.shape[2]
    units = gate_saved.shape[2]
    half = hidden_in.shape[1] // 2

    def mine_theirs(block):
        low, high = block[:half], block[half:]
        return jnp.where(first, low, high), jnp.where(first, high, low)

    def by_layer(own, other):
        return jnp.where(first, other, own), jnp.where(first, own, other)

    gate_blocks = gate_saved[0].reshape(2, 2, half, units)
    up_blocks = up_saved[0].reshape(2, 2, half, units)
    saved = jnp.stack([gate_blocks, up_blocks])
    saved_low, saved_high = saved[:, :, 0], saved[:, :, 1]
    saved_mine = jnp.where(first, saved_low, saved_high)
    saved_other = swap(jnp.where(first, saved_high, saved_low))

    def gather_saved(block):
        block = block.reshape(2, 1, 2 * half, units)
        return lax.all_gather(block, "row", axis=2, tiled=True)

    saved1, saved0 = by_layer(saved_mine, saved_other)
    down_own = w_down[0]
    down_swapped = swap(after(down_own, saved_other))
    down1 = after(jnp.where(first, down_swapped, down_own), saved1)
    hid_mine, hid_theirs = mine_theirs(hidden_in[0])
    hid_other = swap(hid_theirs)
    gain1, gain0 = by_layer(norm_gain[0], swap(norm_gain[0]))
    hid1, hid0 = by_layer(hid_mine, hid_other)

    def scatter_units(cot, down_w):
        cot_all = spread(cot, "col").reshape(cols * half, features)
        return cot_all, dot(cot_all, down_w, ((1,), (1,))).astype(bf16)

    def gather_units(partial):
        pieces = exchange(partial.reshape(rows, 2 * half, units), "row")
        return jnp.sum(pieces.astype(f32), axis=0).astype(bf16)

    def all_units(grad_local):
        return spread(grad_local, "row").reshape(cols * half, units)

    def normed_grads(partial):
        pieces = exchange(partial.reshape(cols, half, features), "col")
        return jnp.sum(pieces.astype(f32), axis=0)

    def inner(normed_grad, hidden, gain):
        return jnp.sum(gain * normed_grad * hidden.astype(f32), axis=1)

    def over_rows(sums):
        return jnp.sum(spread(sums.reshape(1, -1), "row"), axis=0)[0]

    def finish(cot, normed_grad, hidden, inv_rms, gain, cross):
        return (
            cot.astype(f32)
            + inv_rms[:, None] * gain * normed_grad
            - hidden.astype(f32) * (inv_rms**3 * cross / D)[:, None]
        ).astype(bf16)

    def gain_part(normed_grad, hidden, inv_rms):
        return jnp.sum(normed_grad * hidden.astype(f32) * inv_rms[:, None], axis=0)

    def activation(saved):
        gate_f = saved[0].astype(f32)
        return (gate_f * jax.nn.sigmoid(gate_f) * saved[1].astype(f32)).astype(bf16)

    def both_halves(layer1, layer0, event):
        layer1, layer0, _ = lax.optimization_barrier((layer1, layer0, event))
        own = jnp.where(first, layer0, layer1)
        other = swap(jnp.where(first, layer1, layer0))
        return own, other

    def handed(block, source, target):
        return lax.ppermute(block, "section", [(source, target)])

    saved1 = gather_saved(saved1)
    cot1 = mine_theirs(out_grad)[0]
    cot_all1, partial = scatter_units(cot1, down1)
    gate_own, up_own = w_gate[0], w_up[0]
    gate_swapped = swap(after(gate_own, cot_all1))
    up_swapped = swap(after(up_own, cot_all1))
    grad_local = gather_units(partial)
    gates1 = lax.optimization_barrier(jnp.where(first, gate_swapped, gate_own))
    ups1 = lax.optimization_barrier(jnp.where(first, up_swapped, up_own))
    both = jnp.concatenate([hid_mine, hid_theirs, hid_other], axis=0).astype(f32)
    squares = after(jnp.sum(both * both, axis=1), grad_local)

    grad_local = after(grad_local, saved1)
    hidden_grad1 = all_units(grad_local)
    gate_grad1, up_grad1 = unit_grads(hidden_grad1, saved1[:, 0])
    partial = into_features(gate_grad1, up_grad1, gates1, ups1)
    saved0 = gather_saved(after(saved0, gate_grad1))
    normed_grad1 = normed_grads(partial)
    sums = over_rows(jnp.concatenate([squares, inner(normed_grad1, hid1, gain1)]))
    inv = lax.rsqrt(sums[: 3 * half] / D + EPSILON)
    inv1, inv0 = by_layer(inv[:half], inv[2 * half :])
    result1 = finish(cot1, normed_grad1, hid1, inv1, gain1, sums[3 * half :])

    down0 = jnp.where(first, *lax.optimization_barrier((down_own, down_swapped, result1))[:2])
    cot_all0, partial = scatter_units(result1, lax.optimization_barrier(down0))
    partial = after(partial, saved0)
    normed = jnp.concatenate([hid_mine, hid_theirs], axis=0).astype(f32)
    normed = normed * inv[: 2 * half, None] * norm_gain[0]
    normed = after(normed.astype(bf16).reshape(2, half, features), cot_all0)
    normed = lax.all_gather(normed, "col", axis=1, tiled=True)
    grad_local = gather_units(partial)
    hidden_grad0 = all_units(grad_local)
    grad_late = handed(hidden_grad0, 1, 0)
    saved_own, saved_theirs = both_halves(saved1[:, 0], saved0[:, 0], cot_all0)
    cot_own, cot_theirs = both_halves(cot_all1, cot_all0, cot_all0)
    grad_early = handed(after(hidden_grad1, cot_all0), 0, 1)
    weights = lax.optimization_barrier((gate_own, gate_swapped, up_own, up_swapped, grad_local))
    gates0 = lax.optimization_barrier(jnp.where(first, weights[0], weights[1]))
    ups0 = lax.optimization_barrier(jnp.where(first, weights[2], weights[3]))
    ready = (saved_theirs, cot_theirs, grad_early, gates0, ups0)
    gate_grad0, up_grad0 = unit_grads(after(hidden_grad0, ready), saved0[:, 0])
    partial = after(into_features(gate_grad0, up_grad0, gates0, ups0), normed)
    normed_grad0 = normed_grads(partial)
    grad_theirs = after(jnp.where(first, grad_late, grad_early), partial)
    gate_theirs, up_theirs = unit_grads(grad_theirs, saved_theirs)
    gate_own, up_own = after(
        (jnp.where(first, gate_grad0, gate_grad1), jnp.where(first, up_grad0, up_grad1)), partial
    )
    gate_grads = jnp.concatenate([gate_own, gate_theirs], axis=0)
    up_grads = jnp.concatenate([up_own, up_theirs], axis=0)
    saved_own, saved_late, cot_own, cot_theirs = after((saved_own, saved_theirs, cot_own, cot_theirs), normed_grad0)
    acts = jnp.concatenate([activation(saved_own), activation(saved_late)], axis=0)
    grad_down = dot(acts, jnp.concatenate([cot_own, cot_theirs], axis=0), ((0,), (0,))).astype(bf16)
    cross = inner(normed_grad0, hid0, gain0)
    for bit in (1, 2, 4):
        cross = cross + lax.ppermute(cross, "row", [(i, i ^ bit) for i in range(rows)])
    result0 = finish(result1, normed_grad0, hid0, inv0, gain0, cross)

    tokens = 2 * half * cols
    normed = normed.reshape(tokens, features)
    grad_gate = dot(normed, gate_grads, ((0,), (0,))).astype(bf16)
    grad_up = dot(normed, up_grads, ((0,), (0,))).astype(bf16)

    gain1_part = gain_part(normed_grad1, hid1, inv1)
    gain0_part = gain_part(normed_grad0, hid0, inv0)
    gain_parts = jnp.stack([jnp.where(first, gain0_part, gain1_part), jnp.where(first, gain1_part, gain0_part)])
    gain_parts = jnp.sum(after(spread(gain_parts, "col"), grad_down), axis=0)
    gain_total = gain_parts[0] + swap(gain_parts[1])
    own = jnp.where(first, result0, result1)
    other = swap(jnp.where(first, result1, result0))
    result = jnp.where(first, jnp.concatenate([own, other]), jnp.concatenate([other, own]))
    return (result[None], gain_total[None], grad_gate[None], grad_up[None], grad_down[None])


def solution(mesh):
    placed = (
        P("section", "col", "row"),
        P("section", "row"),
        P("section", "row", "col"),
        P("section", "row", "col"),
        P("section", "row", "col"),
        P("section", "row", "col"),
        P("section", "col", "row"),
        P("col", "row"),
    )
    return jax.shard_map(
        body,
        mesh=mesh,
        in_specs=placed,
        out_specs=(
            P("section", "col", "row"),
            P("section", "row"),
            P("section", "row", "col"),
            P("section", "row", "col"),
            P("section", "col", "row"),
        ),
        check_vma=False,
    )
```

profile of v0, /device:TPU:1, one launch (start us, length us, event | category | flops | bytes accessed | tf_op | source)
XLA Modules:
  0.0 294.9 jit_solution(9763070227089222449)
XLA Ops:
  7.2 1.1 fusion.65
  8.3 3.3 %collective-permute-start.1 = (bf16[2,2,32,896]{3,2,1,0:T(8,128)(2,1)S(1)}, bf16[2,2,32,896]{3,2,1,0:T(8,128)(2,1)S(1)}, u32[]{:S(2)}, u32[]{:S(2)}) collective-permute-start(bf16[2,2,32,896]{3,2,1,0:T(8,128)(2,1)S(1)} %fusion.65), channel_id=1, source_target_pairs={{0,128},{128,0},{1,129},{129,1},{2,130},{130,2},{3,131},{131,3},{4... | collective-permute-start | bytes 688136 | tf_op jit(solution)/shard_map/ppermute | solution.py:18
  11.7 1.1 collective-permute-done.1
  13.2 2.0 broadcast_select_fusion.13
  15.3 1.1 broadcast_in_dim.20
  16.4 5.0 %all-to-all-start = ((bf16[16,32,1024]{2,1,0:T(8,128)(2,1)}), bf16[16,32,1024]{2,1,0:T(8,128)(2,1)S(1)}, u32[]{:S(2)}, u32[]{:S(2)}) async-start(bf16[16,32,1024]{2,1,0:T(8,128)(2,1)} %broadcast_in_dim.20), calls=%async_computation | async-start | bytes 2097152 | tf_op jit(solution)/shard_map/all_to_all | solution.py:26
  21.4 1.4 broadcast_select_fusion.7
  22.8 15.3 %all-to-all-done = bf16[16,32,1024]{2,1,0:T(8,128)(2,1)S(1)} async-done(((bf16[16,32,1024]{2,1,0:T(8,128)(2,1)}), bf16[16,32,1024]{2,1,0:T(8,128)(2,1)S(1)}, u32[]{:S(2)}, u32[]{:S(2)}) %all-to-all-start) | async-done | bytes 1048608 | tf_op jit(solution)/shard_map/all_to_all | solution.py:26
  38.1 3.7 %convolution_convert_fusion.1 = bf16[512,896]{1,0:T(8,128)(2,1)} fusion(bf16[512,1024]{1,0:T(8,128)(2,1)S(1)} %bitcast.159, bf16[896,1024]{1,0:T(8,128)(2,1)} %broadcast_select_fusion.7), kind=kOutput, calls=%fused_computation.84 | convolution fusion | flops 939982848 | bytes 3801088 | tf_op jit(solution)/shard_map/dot_general | solution.py:14
  41.9 8.2 %all-to-all-start.1 = ((bf16[8,64,896]{2,1,0:T(8,128)(2,1)}), bf16[8,64,896]{2,1,0:T(8,128)(2,1)}, u32[]{:S(2)}, u32[]{:S(2)}) async-start(bf16[8,64,896]{2,1,0:T(8,128)(2,1)} %bitcast.164), calls=%async_computation.1 | async-start | bytes 1835008 | tf_op jit(solution)/shard_map/all_to_all | solution.py:26
  50.0 2.1 collective-permute-start.5
  52.3 22.6 %all-to-all-done.1 = bf16[8,64,896]{2,1,0:T(8,128)(2,1)} async-done(((bf16[8,64,896]{2,1,0:T(8,128)(2,1)}), bf16[8,64,896]{2,1,0:T(8,128)(2,1)}, u32[]{:S(2)}, u32[]{:S(2)}) %all-to-all-start.1) | async-done | bytes 917536 | tf_op jit(solution)/shard_map/all_to_all | solution.py:26
  74.9 1.3 reduce_sum.108
  76.2 1.0 broadcast_in_dim.21
  77.3 4.2 %all-to-all-start.2 = ((bf16[8,64,896]{2,1,0:T(8,128)(2,1)}), bf16[8,64,896]{2,1,0:T(8,128)(2,1)}, u32[]{:S(2)}, u32[]{:S(2)}) async-start(bf16[8,64,896]{2,1,0:T(8,128)(2,1)} %broadcast_in_dim.21), calls=%async_computation.2 | async-start | bytes 1835008 | tf_op jit(solution)/shard_map/all_to_all | solution.py:26
  81.5 3.1 %broadcast_select_fusion.4 = bf16[1024,896]{1,0:T(8,128)(2,1)} fusion(bf16[1024,896]{1,0:T(8,128)(2,1)} %collective-permute-done.5, pred[]{:T(512)S(6)} %eq.3, bf16[1,1024,896]{2,1,0:T(8,128)(2,1)} %param.13), kind=kLoop, calls=%fused_computation.78 | loop fusion | flops 917504 | bytes 5505025 | tf_op jit(solution)/shard_map/jit(_where)/select_n | solution.py:134
  84.6 1.4 broadcast_select_fusion.5
  86.0 21.9 %all-to-all-done.2 = bf16[8,64,896]{2,1,0:T(8,128)(2,1)} async-done(((bf16[8,64,896]{2,1,0:T(8,128)(2,1)}), bf16[8,64,896]{2,1,0:T(8,128)(2,1)}, u32[]{:S(2)}, u32[]{:S(2)}) %all-to-all-start.2) | async-done | bytes 917536 | tf_op jit(solution)/shard_map/all_to_all | solution.py:26
  107.9 2.8 fusion.6
  110.7 1.3 fusion.90
  112.0 0.8 copy-done.11
  112.9 2.3 add_convert_fusion.1
  115.1 6.2 %all-to-all-start.3 = ((bf16[16,32,1024]{2,1,0:T(8,128)(2,1)}), bf16[16,32,1024]{2,1,0:T(8,128)(2,1)}, u32[]{:S(2)}, u32[]{:S(2)}) async-start(bf16[16,32,1024]{2,1,0:T(8,128)(2,1)} %bitcast.161), calls=%async_computation.3 | async-start | bytes 2097152 | tf_op jit(solution)/shard_map/all_to_all | solution.py:26
  122.1 0.9 collective-permute-start.3
  123.8 13.8 %all-to-all-done.3 = bf16[16,32,1024]{2,1,0:T(8,128)(2,1)} async-done(((bf16[16,32,1024]{2,1,0:T(8,128)(2,1)}), bf16[16,32,1024]{2,1,0:T(8,128)(2,1)}, u32[]{:S(2)}, u32[]{:S(2)}) %all-to-all-start.3) | async-done | bytes 1048608 | tf_op jit(solution)/shard_map/all_to_all | solution.py:26
  137.6 1.4 convert_reduce_fusion.1
  139.0 0.8 fusion.66
  140.0 9.0 %all_to_all.50 = f32[8,1,128]{2,1,0:T(1,128)S(1)} all-to-all(f32[8,1,128]{2,1,0:T(1,128)S(1)} %broadcast_in_dim.22), channel_id=1, replica_groups=mesh['section'=2,'row'=8,'col'=16] {'row'}, dimensions={0} | all-to-all | bytes 8192 | tf_op jit(solution)/shard_map/all_to_all | solution.py:26
  149.1 1.0 fusion.70
  150.1 1.1 broadcast_in_dim.23
  151.2 4.5 %all-to-all-start.5 = ((bf16[16,32,1024]{2,1,0:T(8,128)(2,1)}), bf16[16,32,1024]{2,1,0:T(8,128)(2,1)}, u32[]{:S(2)}, u32[]{:S(2)}) async-start(bf16[16,32,1024]{2,1,0:T(8,128)(2,1)} %broadcast_in_dim.23), calls=%async_computation.5 | async-start | bytes 2097152 | tf_op jit(solution)/shard_map/all_to_all | solution.py:26
  155.7 2.9 broadcast_select_fusion.6
  158.6 11.1 %all-to-all-done.5 = bf16[16,32,1024]{2,1,0:T(8,128)(2,1)} async-done(((bf16[16,32,1024]{2,1,0:T(8,128)(2,1)}), bf16[16,32,1024]{2,1,0:T(8,128)(2,1)}, u32[]{:S(2)}, u32[]{:S(2)}) %all-to-all-start.5) | async-done | bytes 1048608 | tf_op jit(solution)/shard_map/all_to_all | solution.py:26
  169.7 4.0 %convolution_convert_fusion = bf16[512,896]{1,0:T(8,128)(2,1)} fusion(bf16[512,1024]{1,0:T(8,128)(2,1)} %bitcast.27, bf16[896,1024]{1,0:T(8,128)(2,1)} %broadcast_select_fusion.6), kind=kOutput, calls=%fused_computation.83 | convolution fusion | flops 939982848 | bytes 3801088 | tf_op jit(solution)/shard_map/dot_general | solution.py:14
  173.7 4.4 %all-to-all-start.6 = ((bf16[8,64,896]{2,1,0:T(8,128)(2,1)}), bf16[8,64,896]{2,1,0:T(8,128)(2,1)}, u32[]{:S(2)}, u32[]{:S(2)}) async-start(bf16[8,64,896]{2,1,0:T(8,128)(2,1)} %bitcast.163), calls=%async_computation.6 | async-start | bytes 1835008 | tf_op jit(solution)/shard_map/all_to_all | solution.py:26
  178.5 0.8 fusion.62
  179.3 3.7 %broadcast_select_fusion = (bf16[2,512,896]{2,1,0:T(8,128)(2,1)}, bf16[2,512,896]{2,1,0:T(8,128)(2,1)}) fusion(bf16[2,512,896]{2,1,0:T(8,128)(2,1)} %bitcast.157, bf16[2,512,896]{2,1,0:T(8,128)(2,1)S(1)} %bitcast.156, pred[]{:T(512)S(6)} %eq.3), kind=kLoop, calls=%fused_computation.74 | loop fusion | flops 1835008 | bytes 7340033 | tf_op jit(solution)/shard_map/jit(_where)/select_n | solution.py:119
  182.9 4.6 %collective-permute-start.6 = (bf16[2,512,896]{2,1,0:T(8,128)(2,1)}, bf16[2,512,896]{2,1,0:T(8,128)(2,1)S(1)}, u32[]{:S(2)}, u32[]{:S(2)}) collective-permute-start(bf16[2,512,896]{2,1,0:T(8,128)(2,1)} %get-tuple-element.76), channel_id=1, source_target_pairs={{0,128},{128,0},{1,129},{129,1},{2,130},{130,2},{3,131},{131,3},{4... | collective-permute-start | bytes 5505032 | tf_op jit(solution)/shard_map/ppermute | solution.py:18
  187.5 13.2 %all-to-all-done.6 = bf16[8,64,896]{2,1,0:T(8,128)(2,1)} async-done(((bf16[8,64,896]{2,1,0:T(8,128)(2,1)}), bf16[8,64,896]{2,1,0:T(8,128)(2,1)}, u32[]{:S(2)}, u32[]{:S(2)}) %all-to-all-start.6) | async-done | bytes 917536 | tf_op jit(solution)/shard_map/all_to_all | solution.py:26
  200.7 1.3 reduce_sum.113
  202.0 1.1 broadcast_in_dim.24
  203.1 4.2 %all-to-all-start.7 = ((bf16[8,64,896]{2,1,0:T(8,128)(2,1)}), bf16[8,64,896]{2,1,0:T(8,128)(2,1)}, u32[]{:S(2)}, u32[]{:S(2)}) async-start(bf16[8,64,896]{2,1,0:T(8,128)(2,1)} %broadcast_in_dim.24), calls=%async_computation.7 | async-start | bytes 1835008 | tf_op jit(solution)/shard_map/all_to_all | solution.py:26
  207.4 2.9 broadcast_select_fusion.8
  210.3 4.3 %collective-permute-start.7 = (bf16[512,1024]{1,0:T(8,128)(2,1)}, bf16[512,1024]{1,0:T(8,128)(2,1)}, u32[]{:S(2)}, u32[]{:S(2)}) collective-permute-start(bf16[512,1024]{1,0:T(8,128)(2,1)} %get-tuple-element.83), channel_id=1, source_target_pairs={{0,128},{128,0},{1,129},{129,1},{2,130},{130,2},{3,131},{131,3},{4... | collective-permute-start | bytes 3145736 | tf_op jit(solution)/shard_map/ppermute | solution.py:18
  214.6 1.3 collective-permute-start.8
  216.0 4.4 %broadcast_select_fusion.2 = (bf16[1024,896]{1,0:T(8,128)(2,1)}, bf16[1024,896]{1,0:T(8,128)(2,1)}) fusion(bf16[1024,896]{1,0:T(8,128)(2,1)S(1)} %bitcast.152, bf16[1024,896]{1,0:T(8,128)(2,1)} %collective-permute-done.5, pred[]{:T(512)S(6)} %eq.3, bf16[1024,896]{1,0:T(8,128)(2,1)S(1)} %bitcast.154, bf16[1024,896]{1,0:T(8,128)(2,1)} %collective-permute-done.4), kind=kLoop, calls=%fused_computation.76 | loop fusion | flops 1835008 | bytes 11010049 | tf_op jit(solution)/shard_map/jit(_where)/select_n | solution.py:164
  220.4 9.7 %all-to-all-done.7 = bf16[8,64,896]{2,1,0:T(8,128)(2,1)} async-done(((bf16[8,64,896]{2,1,0:T(8,128)(2,1)}), bf16[8,64,896]{2,1,0:T(8,128)(2,1)}, u32[]{:S(2)}, u32[]{:S(2)}) %all-to-all-start.7) | async-done | bytes 917536 | tf_op jit(solution)/shard_map/all_to_all | solution.py:26
  230.1 7.1 %collective-permute-start.14 = (bf16[512,896]{1,0:T(8,128)(2,1)}, bf16[512,896]{1,0:T(8,128)(2,1)}, u32[]{:S(2)}, u32[]{:S(2)}) collective-permute-start(bf16[512,896]{1,0:T(8,128)(2,1)} %bitcast.30), channel_id=1, source_target_pairs={{128,0},{129,1},{130,2},{131,3},{132,4},{133,5},{134,6},{135,7},{1... | collective-permute-start | bytes 2752520 | tf_op jit(solution)/shard_map/ppermute | solution.py:124
  237.2 4.6 %broadcast_select_fusion.12 = (bf16[512,896]{1,0:T(8,128)(2,1)}, bf16[512,896]{1,0:T(8,128)(2,1)S(1)}, bf16[512,896]{1,0:T(8,128)(2,1)}) fusion(bf16[512,896]{1,0:T(8,128)(2,1)S(1)} %copy-done.8, pred[]{:T(512)S(6)} %eq.3, bf16[2,1,512,896]{3,2,0,1:T(8,128)(2,1)} %all-gather.6.cloned.1.call-done, bf16[2,1,512,896]{3,2,1,0:T(8,128)(2,1)} %bitcast.158, ...), kind=kLoop, calls=%fused_computation.95 | loop fusion | flops 8257536 | bytes 7340033 | tf_op jit(solution)/shard_map/jit(_where)/select_n | solution.py:172
  241.8 2.6 fusion.85
  244.5 2.3 add_convert_fusion
  246.8 4.3 %all-to-all-start.8 = ((bf16[16,32,1024]{2,1,0:T(8,128)(2,1)}), bf16[16,32,1024]{2,1,0:T(8,128)(2,1)S(1)}, u32[]{:S(2)}, u32[]{:S(2)}) async-start(bf16[16,32,1024]{2,1,0:T(8,128)(2,1)} %bitcast.162), calls=%async_computation.8 | async-start | bytes 2097152 | tf_op jit(solution)/shard_map/all_to_all | solution.py:26
  251.1 1.3 broadcast_select_fusion.10
  252.4 1.0 fusion.38
  254.3 3.6 %convert_bitcast_fusion.1 = bf16[1,1024,896]{2,1,0:T(8,128)(2,1)} fusion(bf16[1024,1024]{1,0:T(8,128)(2,1)S(1)} %bitcast.184, bf16[512,896]{1,0:T(8,128)(2,1)S(1)} %get-tuple-element.78, bf16[512,896]{1,0:T(8,128)(2,1)S(1)} %copy-done.16), kind=kOutput, calls=%fused_computation.71 | convolution fusion | flops 1883635712 | bytes 5767168 | tf_op jit(solution)/shard_map/dot_general | solution.py:14
  258.0 3.7 %convert_bitcast_fusion = bf16[1,1024,896]{2,1,0:T(8,128)(2,1)} fusion(bf16[1024,1024]{1,0:T(8,128)(2,1)S(1)} %bitcast.185, bf16[512,896]{1,0:T(8,128)(2,1)S(1)} %get-tuple-element.77, bf16[512,896]{1,0:T(8,128)(2,1)S(1)} %copy-done.15), kind=kOutput, calls=%fused_computation.70 | convolution fusion | flops 1883635712 | bytes 5767168 | tf_op jit(solution)/shard_map/dot_general | solution.py:14
  261.6 6.2 %all-to-all-done.8 = bf16[16,32,1024]{2,1,0:T(8,128)(2,1)S(1)} async-done(((bf16[16,32,1024]{2,1,0:T(8,128)(2,1)}), bf16[16,32,1024]{2,1,0:T(8,128)(2,1)S(1)}, u32[]{:S(2)}, u32[]{:S(2)}) %all-to-all-start.8) | async-done | bytes 1048608 | tf_op jit(solution)/shard_map/all_to_all | solution.py:26
  269.2 3.5 %all-to-all-start.9 = ((f32[16,2,1024]{2,1,0:T(2,128)}), f32[16,2,1024]{2,1,0:T(2,128)S(1)}, u32[]{:S(2)}, u32[]{:S(2)}) async-start(f32[16,2,1024]{2,1,0:T(2,128)} %broadcast_in_dim.25), calls=%async_computation.9 | async-start | bytes 262144 | tf_op jit(solution)/shard_map/all_to_all | solution.py:26
  273.5 0.8 copy-done.4
  274.8 1.9 collective-permute-done.10
  276.7 1.1 collective-permute-start.11
  277.8 4.6 %fusion.56 = bf16[896,1024]{1,0:T(8,128)(2,1)} fusion(bf16[512,1024]{1,0:T(8,128)(2,1)} %collective-permute-done.7, bf16[512,1024]{1,0:T(8,128)(2,1)S(1)} %copy-done.14, bf16[512,896]{1,0:T(8,128)(2,1)S(1)} %fusion.50, bf16[512,896]{1,0:T(8,128)(2,1)S(1)} %fusion.51), kind=kOutput, calls=%fused_computation.82 | convolution fusion | flops 1887830016 | bytes 5767168 | tf_op jit(solution)/shard_map/dot_general | solution.py:14
  283.2 3.0 %collective-permute-start.12 = (bf16[32,1024]{1,0:T(8,128)(2,1)S(1)}, bf16[32,1024]{1,0:T(8,128)(2,1)S(1)}, u32[]{:S(2)}, u32[]{:S(2)}) collective-permute-start(bf16[32,1024]{1,0:T(8,128)(2,1)S(1)} %get-tuple-element.87), channel_id=1, source_target_pairs={{0,128},{128,0},{1,129},{129,1},{2,130},{130,2},{3,131},{131,3},{4... | collective-permute-start | bytes 196616 | tf_op jit(solution)/shard_map/ppermute | solution.py:18
  286.4 0.7 collective-permute-done.12
  (96 shorter events, 8.8 us)
Async XLA Ops:
  7.2 8.1 %copy-start.18 = (bf16[64,1024]{1,0:T(8,128)(2,1)S(1)}, bf16[64,1024]{1,0:T(8,128)(2,1)}, u32[]{:S(2)}) copy-start(bf16[64,1024]{1,0:T(8,128)(2,1)} %param.15) | copy-start | bytes 393220
  7.2 69.0 %all-gather.4.cloned.1.call-start = ((), (), s32[]{:S(2)}) async-start(), calls=%async_computation.10 | async-start | bytes 2064384 | tf_op jit(solution)/shard_map/all_gather | solution.py:71
  8.3 4.4 %collective-permute-start.1 = (bf16[2,2,32,896]{3,2,1,0:T(8,128)(2,1)S(1)}, bf16[2,2,32,896]{3,2,1,0:T(8,128)(2,1)S(1)}, u32[]{:S(2)}, u32[]{:S(2)}) collective-permute-start(bf16[2,2,32,896]{3,2,1,0:T(8,128)(2,1)S(1)} %fusion.65), channel_id=1, source_target_pairs={{0,128},{128,0},{1,129},{129,1},{2,130},{130,2},{3,131},{131,3},{4... | collective-permute-start | bytes 688136 | tf_op jit(solution)/shard_map/ppermute | solution.py:18
  12.8 8.6 %collective-permute-start.2 = (bf16[896,1024]{1,0:T(8,128)(2,1)}, bf16[896,1024]{1,0:T(8,128)(2,1)}, u32[]{:S(2)}, u32[]{:S(2)}) collective-permute-start(bf16[896,1024]{1,0:T(8,128)(2,1)} %bitcast.149), channel_id=1, source_target_pairs={{0,128},{128,0},{1,129},{129,1},{2,130},{130,2},{3,131},{131,3},{4... | collective-permute-start | bytes 5505032 | tf_op jit(solution)/shard_map/ppermute | solution.py:18
  15.2 6.2 %copy-start = (bf16[1,896,1024]{2,1,0:T(8,128)(2,1)S(1)}, bf16[1,896,1024]{2,1,0:T(8,128)(2,1)}, u32[]{:S(2)}) copy-start(bf16[1,896,1024]{2,1,0:T(8,128)(2,1)} %param.14) | copy-start | bytes 5505028
  16.4 21.8 %all-to-all-start = ((bf16[16,32,1024]{2,1,0:T(8,128)(2,1)}), bf16[16,32,1024]{2,1,0:T(8,128)(2,1)S(1)}, u32[]{:S(2)}, u32[]{:S(2)}) async-start(bf16[16,32,1024]{2,1,0:T(8,128)(2,1)} %broadcast_in_dim.20), calls=%async_computation | async-start | bytes 2097152 | tf_op jit(solution)/shard_map/all_to_all | solution.py:26
  41.9 33.0 %all-to-all-start.1 = ((bf16[8,64,896]{2,1,0:T(8,128)(2,1)}), bf16[8,64,896]{2,1,0:T(8,128)(2,1)}, u32[]{:S(2)}, u32[]{:S(2)}) async-start(bf16[8,64,896]{2,1,0:T(8,128)(2,1)} %bitcast.164), calls=%async_computation.1 | async-start | bytes 1835008 | tf_op jit(solution)/shard_map/all_to_all | solution.py:26
  50.0 31.5 %collective-permute-start.5 = (bf16[1024,896]{1,0:T(8,128)(2,1)}, bf16[1024,896]{1,0:T(8,128)(2,1)}, u32[]{:S(2)}, u32[]{:S(2)}) collective-permute-start(bf16[1024,896]{1,0:T(8,128)(2,1)} %bitcast.151), channel_id=1, source_target_pairs={{0,128},{128,0},{1,129},{129,1},{2,130},{130,2},{3,131},{131,3},{4... | collective-permute-start | bytes 5505032 | tf_op jit(solution)/shard_map/ppermute | solution.py:18
  52.2 32.4 %collective-permute-start.4 = (bf16[1024,896]{1,0:T(8,128)(2,1)}, bf16[1024,896]{1,0:T(8,128)(2,1)}, u32[]{:S(2)}, u32[]{:S(2)}) collective-permute-start(bf16[1024,896]{1,0:T(8,128)(2,1)} %bitcast.153), channel_id=1, source_target_pairs={{0,128},{128,0},{1,129},{129,1},{2,130},{130,2},{3,131},{131,3},{4... | collective-permute-start | bytes 5505032 | tf_op jit(solution)/shard_map/ppermute | solution.py:18
  77.3 30.6 %all-to-all-start.2 = ((bf16[8,64,896]{2,1,0:T(8,128)(2,1)}), bf16[8,64,896]{2,1,0:T(8,128)(2,1)}, u32[]{:S(2)}, u32[]{:S(2)}) async-start(bf16[8,64,896]{2,1,0:T(8,128)(2,1)} %broadcast_in_dim.21), calls=%async_computation.2 | async-start | bytes 1835008 | tf_op jit(solution)/shard_map/all_to_all | solution.py:26
  81.5 3.1 %copy-start.2 = (bf16[1,1024,896]{2,1,0:T(8,128)(2,1)S(1)}, bf16[1,1024,896]{2,1,0:T(8,128)(2,1)}, u32[]{:S(2)}) copy-start(bf16[1,1024,896]{2,1,0:T(8,128)(2,1)} %param.12) | copy-start | bytes 5505028
  107.9 2.9 copy-start.10
  110.7 1.3 copy-start.9
  110.7 1.3 copy-start.7
  110.7 2.2 copy-start.11
  115.1 6.9 %copy-start.19 = (f32[1,1024]{1,0:T(1,128)S(1)}, f32[1,1024]{1,0:T(1,128)}, u32[]{:S(2)}) copy-start(f32[1,1024]{1,0:T(1,128)} %param.9) | copy-start | bytes 12292
  115.1 7.8 %copy-start.17 = (bf16[1,64,1024]{2,1,0:T(8,128)(2,1)S(1)}, bf16[1,64,1024]{2,1,0:T(8,128)(2,1)}, u32[]{:S(2)}) copy-start(bf16[1,64,1024]{2,1,0:T(8,128)(2,1)} %param.8) | copy-start | bytes 393220
  115.1 22.4 %all-to-all-start.3 = ((bf16[16,32,1024]{2,1,0:T(8,128)(2,1)}), bf16[16,32,1024]{2,1,0:T(8,128)(2,1)}, u32[]{:S(2)}, u32[]{:S(2)}) async-start(bf16[16,32,1024]{2,1,0:T(8,128)(2,1)} %bitcast.161), calls=%async_computation.3 | async-start | bytes 2097152 | tf_op jit(solution)/shard_map/all_to_all | solution.py:26
  121.3 52.4 %all-gather.6.cloned.1.call-start = ((), (), s32[]{:S(2)}) async-start(), calls=%async_computation.11 | async-start | bytes 2064384 | tf_op jit(solution)/shard_map/all_gather | solution.py:71
  122.1 1.7 collective-permute-start.3
  122.9 16.1 %collective-permute-start = (bf16[32,1024]{1,0:T(8,128)(2,1)S(1)}, bf16[32,1024]{1,0:T(8,128)(2,1)S(1)}, u32[]{:S(2)}, u32[]{:S(2)}) collective-permute-start(bf16[32,1024]{1,0:T(8,128)(2,1)S(1)} %select_bitcast_fusion.1), channel_id=1, source_target_pairs={{0,128},{128,0},{1,129},{129,1},{2,130},{130,2},{3,131},{131,3},{4... | collective-permute-start | bytes 196616 | tf_op jit(solution)/shard_map/ppermute | solution.py:18
  151.2 18.5 %all-to-all-start.5 = ((bf16[16,32,1024]{2,1,0:T(8,128)(2,1)}), bf16[16,32,1024]{2,1,0:T(8,128)(2,1)}, u32[]{:S(2)}, u32[]{:S(2)}) async-start(bf16[16,32,1024]{2,1,0:T(8,128)(2,1)} %broadcast_in_dim.23), calls=%async_computation.5 | async-start | bytes 2097152 | tf_op jit(solution)/shard_map/all_to_all | solution.py:26
  173.7 5.5 %copy-start.5 = (bf16[2,1,512,896]{3,2,0,1:T(8,128)(2,1)S(1)}, bf16[2,1,512,896]{3,2,0,1:T(8,128)(2,1)}, u32[]{:S(2)}) copy-start(bf16[2,1,512,896]{3,2,0,1:T(8,128)(2,1)} %all-gather.4.cloned.1.call-done) | copy-start | bytes 5505028
  173.7 27.0 %all-to-all-start.6 = ((bf16[8,64,896]{2,1,0:T(8,128)(2,1)}), bf16[8,64,896]{2,1,0:T(8,128)(2,1)}, u32[]{:S(2)}, u32[]{:S(2)}) async-start(bf16[8,64,896]{2,1,0:T(8,128)(2,1)} %bitcast.163), calls=%async_computation.6 | async-start | bytes 1835008 | tf_op jit(solution)/shard_map/all_to_all | solution.py:26
  178.1 68.7 %all-gather.8.cloned.1.call-start = ((), (), s32[]{:S(2)}) async-start(), calls=%async_computation.12 | async-start | bytes 2228224 | tf_op jit(solution)/shard_map/all_gather | solution.py:155
  182.9 54.2 %collective-permute-start.6 = (bf16[2,512,896]{2,1,0:T(8,128)(2,1)}, bf16[2,512,896]{2,1,0:T(8,128)(2,1)S(1)}, u32[]{:S(2)}, u32[]{:S(2)}) collective-permute-start(bf16[2,512,896]{2,1,0:T(8,128)(2,1)} %get-tuple-element.76), channel_id=1, source_target_pairs={{0,128},{128,0},{1,129},{129,1},{2,130},{130,2},{3,131},{131,3},{4... | collective-permute-start | bytes 5505032 | tf_op jit(solution)/shard_map/ppermute | solution.py:18
  203.1 26.9 %all-to-all-start.7 = ((bf16[8,64,896]{2,1,0:T(8,128)(2,1)}), bf16[8,64,896]{2,1,0:T(8,128)(2,1)}, u32[]{:S(2)}, u32[]{:S(2)}) async-start(bf16[8,64,896]{2,1,0:T(8,128)(2,1)} %broadcast_in_dim.24), calls=%async_computation.7 | async-start | bytes 1835008 | tf_op jit(solution)/shard_map/all_to_all | solution.py:26
  207.4 8.6 %copy-start.1 = (bf16[1,1024,896]{2,1,0:T(8,128)(2,1)S(1)}, bf16[1,1024,896]{2,1,0:T(8,128)(2,1)}, u32[]{:S(2)}) copy-start(bf16[1,1024,896]{2,1,0:T(8,128)(2,1)} %param.13) | copy-start | bytes 5505028
  207.4 8.6 %copy-start.3 = (bf16[1,1024,896]{2,1,0:T(8,128)(2,1)S(1)}, bf16[1,1024,896]{2,1,0:T(8,128)(2,1)}, u32[]{:S(2)}) copy-start(bf16[1,1024,896]{2,1,0:T(8,128)(2,1)} %param.12) | copy-start | bytes 5505028
  210.3 26.9 %collective-permute-start.7 = (bf16[512,1024]{1,0:T(8,128)(2,1)}, bf16[512,1024]{1,0:T(8,128)(2,1)}, u32[]{:S(2)}, u32[]{:S(2)}) collective-permute-start(bf16[512,1024]{1,0:T(8,128)(2,1)} %get-tuple-element.83), channel_id=1, source_target_pairs={{0,128},{128,0},{1,129},{129,1},{2,130},{130,2},{3,131},{131,3},{4... | collective-permute-start | bytes 3145736 | tf_op jit(solution)/shard_map/ppermute | solution.py:18
  214.6 22.6 %collective-permute-start.8 = (bf16[512,896]{1,0:T(8,128)(2,1)}, bf16[512,896]{1,0:T(8,128)(2,1)}, u32[]{:S(2)}, u32[]{:S(2)}) collective-permute-start(bf16[512,896]{1,0:T(8,128)(2,1)} %bitcast.14), channel_id=1, source_target_pairs={{0,128},{1,129},{2,130},{3,131},{4,132},{5,133},{6,134},{7,135},{8... | collective-permute-start | bytes 2752520 | tf_op jit(solution)/shard_map/ppermute | solution.py:124
  215.9 21.2 %copy-start.8 = (bf16[512,896]{1,0:T(8,128)(2,1)S(1)}, bf16[512,896]{1,0:T(8,128)(2,1)}, u32[]{:S(2)}) copy-start(bf16[512,896]{1,0:T(8,128)(2,1)} %copy-done.7) | copy-start | bytes 2752516
  230.1 21.0 %collective-permute-start.14 = (bf16[512,896]{1,0:T(8,128)(2,1)}, bf16[512,896]{1,0:T(8,128)(2,1)}, u32[]{:S(2)}, u32[]{:S(2)}) collective-permute-start(bf16[512,896]{1,0:T(8,128)(2,1)} %bitcast.30), channel_id=1, source_target_pairs={{128,0},{129,1},{130,2},{131,3},{132,4},{133,5},{134,6},{135,7},{1... | collective-permute-start | bytes 2752520 | tf_op jit(solution)/shard_map/ppermute | solution.py:124
  237.2 4.6 %copy-start.6 = (bf16[2,1,512,896]{3,2,0,1:T(8,128)(2,1)S(1)}, bf16[2,1,512,896]{3,2,0,1:T(8,128)(2,1)}, u32[]{:S(2)}) copy-start(bf16[2,1,512,896]{3,2,0,1:T(8,128)(2,1)} %all-gather.6.cloned.1.call-done) | copy-start | bytes 5505028
  237.2 4.6 %copy-start.13 = (bf16[1024,896]{1,0:T(8,128)(2,1)S(1)}, bf16[1024,896]{1,0:T(8,128)(2,1)}, u32[]{:S(2)}) copy-start(bf16[1024,896]{1,0:T(8,128)(2,1)} %get-tuple-element.96) | copy-start | bytes 5505028
  241.8 2.7 copy-start.12
  246.8 21.0 %all-to-all-start.8 = ((bf16[16,32,1024]{2,1,0:T(8,128)(2,1)}), bf16[16,32,1024]{2,1,0:T(8,128)(2,1)S(1)}, u32[]{:S(2)}, u32[]{:S(2)}) async-start(bf16[16,32,1024]{2,1,0:T(8,128)(2,1)} %bitcast.162), calls=%async_computation.8 | async-start | bytes 2097152 | tf_op jit(solution)/shard_map/all_to_all | solution.py:26
  252.4 1.2 copy-start.16
  252.4 1.9 copy-start.20
  254.3 3.7 %copy-start.15 = (bf16[512,896]{1,0:T(8,128)(2,1)S(1)}, bf16[512,896]{1,0:T(8,128)(2,1)}, u32[]{:S(2)}) copy-start(bf16[512,896]{1,0:T(8,128)(2,1)} %get-tuple-element.64) | copy-start | bytes 2752516
  268.1 5.2 %collective-permute-start.9 = (f32[32]{0:T(128)S(1)}, f32[32]{0:T(128)S(1)}, u32[]{:S(2)}, u32[]{:S(2)}) collective-permute-start(f32[32]{0:T(128)S(1)} %get-tuple-element.66), channel_id=1, source_target_pairs={{0,16},{16,0},{32,48},{48,32},{64,80},{80,64},{96,112},{112,96},{1... | collective-permute-start | bytes 392 | tf_op jit(solution)/shard_map/ppermute | solution.py:181
  269.2 17.0 %all-to-all-start.9 = ((f32[16,2,1024]{2,1,0:T(2,128)}), f32[16,2,1024]{2,1,0:T(2,128)S(1)}, u32[]{:S(2)}, u32[]{:S(2)}) async-start(f32[16,2,1024]{2,1,0:T(2,128)} %broadcast_in_dim.25), calls=%async_computation.9 | async-start | bytes 262144 | tf_op jit(solution)/shard_map/all_to_all | solution.py:26
  272.7 1.5 copy-start.4
  273.3 4.5 %copy-start.14 = (bf16[512,1024]{1,0:T(8,128)(2,1)S(1)}, bf16[512,1024]{1,0:T(8,128)(2,1)}, u32[]{:S(2)}) copy-start(bf16[512,1024]{1,0:T(8,128)(2,1)} %get-tuple-element.59) | copy-start | bytes 3145732
  273.4 3.4 %collective-permute-start.10 = (f32[32]{0:T(128)S(1)}, f32[32]{0:T(128)S(1)}, u32[]{:S(2)}, u32[]{:S(2)}) collective-permute-start(f32[32]{0:T(128)S(1)} %add.67), channel_id=1, source_target_pairs={{0,32},{16,48},{32,0},{48,16},{64,96},{80,112},{96,64},{112,80},{1... | collective-permute-start | bytes 392 | tf_op jit(solution)/shard_map/ppermute | solution.py:181
  276.7 6.3 %collective-permute-start.11 = (f32[32]{0:T(128)S(1)}, f32[32]{0:T(128)S(1)}, u32[]{:S(2)}, u32[]{:S(2)}) collective-permute-start(f32[32]{0:T(128)S(1)} %add.68), channel_id=1, source_target_pairs={{0,64},{16,80},{32,96},{48,112},{64,0},{80,16},{96,32},{112,48},{1... | collective-permute-start | bytes 392 | tf_op jit(solution)/shard_map/ppermute | solution.py:181
  283.2 3.9 %collective-permute-start.12 = (bf16[32,1024]{1,0:T(8,128)(2,1)S(1)}, bf16[32,1024]{1,0:T(8,128)(2,1)S(1)}, u32[]{:S(2)}, u32[]{:S(2)}) collective-permute-start(bf16[32,1024]{1,0:T(8,128)(2,1)S(1)} %get-tuple-element.87), channel_id=1, source_target_pairs={{0,128},{128,0},{1,129},{129,1},{2,130},{130,2},{3,131},{131,3},{4... | collective-permute-start | bytes 196616 | tf_op jit(solution)/shard_map/ppermute | solution.py:18
  286.3 1.5 collective-permute-start.13
Sparse Core Ops, SparseCore 0:
  15.3 37.7 all-gather.3
  123.9 33.5 all-gather.5
  182.0 50.7 all-gather.7
where the time goes:
time: 296 us; the launch traced here: 295 us
  waiting for transfers between devices  120 us (41%)
  starting transfers between devices  73.7 us (25%)
  other arithmetic  42.7 us (14%)
  matrix products  28.1 us (9%)
  between operations  14.2 us (5%)
  blocking collectives  8.98 us (3%)
  local copies, waits for them, and re-layouts  7.73 us (3%)
    all_to_all x9, waiting for transfers between devices, exchange(): return lax.all_to_all(blocks, axis, 0, 0)  114 us
    all_to_all x9, starting transfers between devices, exchange(): return lax.all_to_all(blocks, axis, 0, 0)  44.6 us
    dot_general x9, matrix products, dot(): lax.dot_general(left, right, (dims, ((), ())), preferred_element_type=f32)  28.1 us
    ppermute x10, starting transfers between devices, swap(): return lax.ppermute(block, 'section', [(0, 1), (1, 0)])  18.9 us
    all_to_all x1, blocking collectives, exchange(): return lax.all_to_all(blocks, axis, 0, 0)  8.98 us
    ppermute x2, starting transfers between devices, handed(): return lax.ppermute(block, 'section', [(source, target)])  8.35 us
    select_n x2, other arithmetic, both_halves(): own = jnp.where(first, layer0, layer1)  6.55 us
  transfers between devices with their start and end apart: 27, of which 13 were waited for; matrix products, arithmetic and copies ran while one was open for 23% of the time, Pallas kernels for 0%

commit v1 on v0

--- a/solution.py
+++ b/solution.py
@@ -168,17 +168,17 @@
     normed_grad0 = normed_grads(partial)
     grad_theirs = after(jnp.where(first, grad_late, grad_early), partial)
     gate_theirs, up_theirs = unit_grads(grad_theirs, saved_theirs)
-    gate_own, up_own = after(
-        (jnp.where(first, gate_grad0, gate_grad1), jnp.where(first, up_grad0, up_grad1)), partial
-    )
+    gate0, gate1, up0, up1 = after((gate_grad0, gate_grad1, up_grad0, up_grad1), partial)
+    gate_own, up_own = jnp.where(first, gate0, gate1), jnp.where(first, up0, up1)
     gate_grads = jnp.concatenate([gate_own, gate_theirs], axis=0)
     up_grads = jnp.concatenate([up_own, up_theirs], axis=0)
     saved_own, saved_late, cot_own, cot_theirs = after((saved_own, saved_theirs, cot_own, cot_theirs), normed_grad0)
     acts = jnp.concatenate([activation(saved_own), activation(saved_late)], axis=0)
     grad_down = dot(acts, jnp.concatenate([cot_own, cot_theirs], axis=0), ((0,), (0,))).astype(bf16)
     cross = inner(normed_grad0, hid0, gain0)
-    for bit in (1, 2, 4):
-        cross = cross + lax.ppermute(cross, "row", [(i, i ^ bit) for i in range(rows)])
+    others = [lax.ppermute(cross, "row", [(i, i ^ bits) for i in range(rows)]) for bits in (1, 2, 3)]
+    cross = cross + others[0] + others[1] + others[2]
+    cross = cross + lax.ppermute(cross, "row", [(i, i ^ 4) for i in range(rows)])
     result0 = finish(result1, normed_grad0, hid0, inv0, gain0, cross)
 
     tokens = 2 * half * cols

time: 296 us -> 295 us (level)
  waiting for transfers between devices: 120 us -> 117 us
    select_n x1 -> x2, other arithmetic: 4.62 us -> 1.52 us  [the longest x1 1.42 us: body(): jnp.where(first, up0, up1)]
    convert_element_type x1 -> x2, other arithmetic: 2.83 us -> 5.88 us  [unit_grads(): (grad_f * up_f * sig * (1.0 + gate_f * (1.0 - sig))).astype(bf16)]
  transfers between devices with their start and end apart: 27 -> 28, of which waited for: 13 -> 12; matrix products, arithmetic and copies ran while one was open for 23% -> 22% of each run, Pallas kernels for 0% -> 0%
where the time goes in v1:
time: 295 us; the launch traced here: 294 us
  waiting for transfers between devices  117 us (40%)
  starting transfers between devices  75.4 us (26%)
  other arithmetic  42.3 us (14%)
  matrix products  27 us (9%)
  between operations  14.2 us (5%)
  blocking collectives  8.98 us (3%)
  local copies, waits for them, and re-layouts  8.8 us (3%)
    all_to_all x9, waiting for transfers between devices, exchange(): return lax.all_to_all(blocks, axis, 0, 0)  113 us
    all_to_all x9, starting transfers between devices, exchange(): return lax.all_to_all(blocks, axis, 0, 0)  44.6 us
    dot_general x9, matrix products, dot(): lax.dot_general(left, right, (dims, ((), ())), preferred_element_type=f32)  27 us
    ppermute x10, starting transfers between devices, swap(): return lax.ppermute(block, 'section', [(0, 1), (1, 0)])  18.3 us
    all_to_all x1, blocking collectives, exchange(): return lax.all_to_all(blocks, axis, 0, 0)  8.98 us
    ppermute x2, starting transfers between devices, handed(): return lax.ppermute(block, 'section', [(source, target)])  8.36 us
    select_n x2, other arithmetic, both_halves(): own = jnp.where(first, layer0, layer1)  6.54 us
  transfers between devices with their start and end apart: 28, of which 12 were waited for; matrix products, arithmetic and copies ran while one was open for 22% of the time, Pallas kernels for 0%

profile of v1, /device:TPU:1, one launch (start us, length us, event | category | flops | bytes accessed | tf_op | source)
XLA Modules:
  0.0 293.5 jit_solution(12558382006684766742)
XLA Ops:
  7.2 1.1 fusion.65
  8.3 3.3 %collective-permute-start.1 = (bf16[2,2,32,896]{3,2,1,0:T(8,128)(2,1)S(1)}, bf16[2,2,32,896]{3,2,1,0:T(8,128)(2,1)S(1)}, u32[]{:S(2)}, u32[]{:S(2)}) collective-permute-start(bf16[2,2,32,896]{3,2,1,0:T(8,128)(2,1)S(1)} %fusion.65), channel_id=1, source_target_pairs={{0,128},{128,0},{1,129},{129,1},{2,130},{130,2},{3,131},{131,3},{4... | collective-permute-start | bytes 688136 | tf_op jit(solution)/shard_map/ppermute | solution.py:18
  11.7 1.1 collective-permute-done.1
  13.2 2.0 broadcast_select_fusion.13
  15.3 1.1 broadcast_in_dim.20
  16.4 5.0 %all-to-all-start = ((bf16[16,32,1024]{2,1,0:T(8,128)(2,1)}), bf16[16,32,1024]{2,1,0:T(8,128)(2,1)S(1)}, u32[]{:S(2)}, u32[]{:S(2)}) async-start(bf16[16,32,1024]{2,1,0:T(8,128)(2,1)} %broadcast_in_dim.20), calls=%async_computation | async-start | bytes 2097152 | tf_op jit(solution)/shard_map/all_to_all | solution.py:26
  21.4 1.4 broadcast_select_fusion.7
  22.8 15.3 %all-to-all-done = bf16[16,32,1024]{2,1,0:T(8,128)(2,1)S(1)} async-done(((bf16[16,32,1024]{2,1,0:T(8,128)(2,1)}), bf16[16,32,1024]{2,1,0:T(8,128)(2,1)S(1)}, u32[]{:S(2)}, u32[]{:S(2)}) %all-to-all-start) | async-done | bytes 1048608 | tf_op jit(solution)/shard_map/all_to_all | solution.py:26
  38.1 3.7 %convolution_convert_fusion.1 = bf16[512,896]{1,0:T(8,128)(2,1)} fusion(bf16[512,1024]{1,0:T(8,128)(2,1)S(1)} %bitcast.155, bf16[896,1024]{1,0:T(8,128)(2,1)} %broadcast_select_fusion.7), kind=kOutput, calls=%fused_computation.84 | convolution fusion | flops 939982848 | bytes 3801088 | tf_op jit(solution)/shard_map/dot_general | solution.py:14
  41.9 8.2 %all-to-all-start.1 = ((bf16[8,64,896]{2,1,0:T(8,128)(2,1)}), bf16[8,64,896]{2,1,0:T(8,128)(2,1)}, u32[]{:S(2)}, u32[]{:S(2)}) async-start(bf16[8,64,896]{2,1,0:T(8,128)(2,1)} %bitcast.160), calls=%async_computation.1 | async-start | bytes 1835008 | tf_op jit(solution)/shard_map/all_to_all | solution.py:26
  50.0 2.1 collective-permute-start.5
  52.3 22.6 %all-to-all-done.1 = bf16[8,64,896]{2,1,0:T(8,128)(2,1)} async-done(((bf16[8,64,896]{2,1,0:T(8,128)(2,1)}), bf16[8,64,896]{2,1,0:T(8,128)(2,1)}, u32[]{:S(2)}, u32[]{:S(2)}) %all-to-all-start.1) | async-done | bytes 917536 | tf_op jit(solution)/shard_map/all_to_all | solution.py:26
  74.9 1.3 reduce_sum.108
  76.2 1.0 broadcast_in_dim.21
  77.3 4.2 %all-to-all-start.2 = ((bf16[8,64,896]{2,1,0:T(8,128)(2,1)}), bf16[8,64,896]{2,1,0:T(8,128)(2,1)}, u32[]{:S(2)}, u32[]{:S(2)}) async-start(bf16[8,64,896]{2,1,0:T(8,128)(2,1)} %broadcast_in_dim.21), calls=%async_computation.2 | async-start | bytes 1835008 | tf_op jit(solution)/shard_map/all_to_all | solution.py:26
  81.5 3.1 %broadcast_select_fusion.4 = bf16[1024,896]{1,0:T(8,128)(2,1)} fusion(bf16[1024,896]{1,0:T(8,128)(2,1)} %collective-permute-done.5, pred[]{:T(512)S(6)} %eq.3, bf16[1,1024,896]{2,1,0:T(8,128)(2,1)} %param.13), kind=kLoop, calls=%fused_computation.78 | loop fusion | flops 917504 | bytes 5505025 | tf_op jit(solution)/shard_map/jit(_where)/select_n | solution.py:134
  84.6 1.4 broadcast_select_fusion.5
  86.0 21.9 %all-to-all-done.2 = bf16[8,64,896]{2,1,0:T(8,128)(2,1)} async-done(((bf16[8,64,896]{2,1,0:T(8,128)(2,1)}), bf16[8,64,896]{2,1,0:T(8,128)(2,1)}, u32[]{:S(2)}, u32[]{:S(2)}) %all-to-all-start.2) | async-done | bytes 917536 | tf_op jit(solution)/shard_map/all_to_all | solution.py:26
  107.9 2.8 fusion.6
  110.7 1.3 fusion.87
  112.0 0.8 copy-done.13
  112.9 2.3 add_convert_fusion.1
  115.1 6.2 %all-to-all-start.3 = ((bf16[16,32,1024]{2,1,0:T(8,128)(2,1)}), bf16[16,32,1024]{2,1,0:T(8,128)(2,1)}, u32[]{:S(2)}, u32[]{:S(2)}) async-start(bf16[16,32,1024]{2,1,0:T(8,128)(2,1)} %bitcast.158), calls=%async_computation.3 | async-start | bytes 2097152 | tf_op jit(solution)/shard_map/all_to_all | solution.py:26
  122.1 0.9 collective-permute-start.3
  123.8 13.8 %all-to-all-done.3 = bf16[16,32,1024]{2,1,0:T(8,128)(2,1)} async-done(((bf16[16,32,1024]{2,1,0:T(8,128)(2,1)}), bf16[16,32,1024]{2,1,0:T(8,128)(2,1)}, u32[]{:S(2)}, u32[]{:S(2)}) %all-to-all-start.3) | async-done | bytes 1048608 | tf_op jit(solution)/shard_map/all_to_all | solution.py:26
  137.6 1.4 convert_reduce_fusion.1
  139.0 0.8 fusion.66
  140.0 9.0 %all_to_all.50 = f32[8,1,128]{2,1,0:T(1,128)S(1)} all-to-all(f32[8,1,128]{2,1,0:T(1,128)S(1)} %broadcast_in_dim.22), channel_id=1, replica_groups=mesh['section'=2,'row'=8,'col'=16] {'row'}, dimensions={0} | all-to-all | bytes 8192 | tf_op jit(solution)/shard_map/all_to_all | solution.py:26
  149.1 1.0 fusion.70
  150.1 1.1 broadcast_in_dim.23
  151.2 4.5 %all-to-all-start.5 = ((bf16[16,32,1024]{2,1,0:T(8,128)(2,1)}), bf16[16,32,1024]{2,1,0:T(8,128)(2,1)}, u32[]{:S(2)}, u32[]{:S(2)}) async-start(bf16[16,32,1024]{2,1,0:T(8,128)(2,1)} %broadcast_in_dim.23), calls=%async_computation.5 | async-start | bytes 2097152 | tf_op jit(solution)/shard_map/all_to_all | solution.py:26
  155.7 2.9 broadcast_select_fusion.6
  158.6 11.1 %all-to-all-done.5 = bf16[16,32,1024]{2,1,0:T(8,128)(2,1)} async-done(((bf16[16,32,1024]{2,1,0:T(8,128)(2,1)}), bf16[16,32,1024]{2,1,0:T(8,128)(2,1)}, u32[]{:S(2)}, u32[]{:S(2)}) %all-to-all-start.5) | async-done | bytes 1048608 | tf_op jit(solution)/shard_map/all_to_all | solution.py:26
  169.7 4.0 %convolution_convert_fusion = bf16[512,896]{1,0:T(8,128)(2,1)} fusion(bf16[512,1024]{1,0:T(8,128)(2,1)} %bitcast.27, bf16[896,1024]{1,0:T(8,128)(2,1)} %broadcast_select_fusion.6), kind=kOutput, calls=%fused_computation.83 | convolution fusion | flops 939982848 | bytes 3801088 | tf_op jit(solution)/shard_map/dot_general | solution.py:14
  173.7 4.4 %all-to-all-start.6 = ((bf16[8,64,896]{2,1,0:T(8,128)(2,1)}), bf16[8,64,896]{2,1,0:T(8,128)(2,1)}, u32[]{:S(2)}, u32[]{:S(2)}) async-start(bf16[8,64,896]{2,1,0:T(8,128)(2,1)} %bitcast.159), calls=%async_computation.6 | async-start | bytes 1835008 | tf_op jit(solution)/shard_map/all_to_all | solution.py:26
  179.2 3.7 %broadcast_select_fusion = (bf16[2,512,896]{2,1,0:T(8,128)(2,1)}, bf16[2,512,896]{2,1,0:T(8,128)(2,1)}) fusion(bf16[2,512,896]{2,1,0:T(8,128)(2,1)} %bitcast.153, bf16[2,512,896]{2,1,0:T(8,128)(2,1)S(1)} %bitcast.152, pred[]{:T(512)S(6)} %eq.3), kind=kLoop, calls=%fused_computation.74 | loop fusion | flops 1835008 | bytes 7340033 | tf_op jit(solution)/shard_map/jit(_where)/select_n | solution.py:119
  182.9 4.6 %collective-permute-start.6 = (bf16[2,512,896]{2,1,0:T(8,128)(2,1)}, bf16[2,512,896]{2,1,0:T(8,128)(2,1)S(1)}, u32[]{:S(2)}, u32[]{:S(2)}) collective-permute-start(bf16[2,512,896]{2,1,0:T(8,128)(2,1)} %get-tuple-element.78), channel_id=1, source_target_pairs={{0,128},{128,0},{1,129},{129,1},{2,130},{130,2},{3,131},{131,3},{4... | collective-permute-start | bytes 5505032 | tf_op jit(solution)/shard_map/ppermute | solution.py:18
  187.5 13.2 %all-to-all-done.6 = bf16[8,64,896]{2,1,0:T(8,128)(2,1)} async-done(((bf16[8,64,896]{2,1,0:T(8,128)(2,1)}), bf16[8,64,896]{2,1,0:T(8,128)(2,1)}, u32[]{:S(2)}, u32[]{:S(2)}) %all-to-all-start.6) | async-done | bytes 917536 | tf_op jit(solution)/shard_map/all_to_all | solution.py:26
  200.7 1.3 reduce_sum.113
  202.0 1.0 broadcast_in_dim.24
  203.1 4.2 %all-to-all-start.7 = ((bf16[8,64,896]{2,1,0:T(8,128)(2,1)}), bf16[8,64,896]{2,1,0:T(8,128)(2,1)}, u32[]{:S(2)}, u32[]{:S(2)}) async-start(bf16[8,64,896]{2,1,0:T(8,128)(2,1)} %broadcast_in_dim.24), calls=%async_computation.7 | async-start | bytes 1835008 | tf_op jit(solution)/shard_map/all_to_all | solution.py:26
  207.3 2.9 broadcast_select_fusion.8
  210.2 4.3 %collective-permute-start.7 = (bf16[512,1024]{1,0:T(8,128)(2,1)}, bf16[512,1024]{1,0:T(8,128)(2,1)}, u32[]{:S(2)}, u32[]{:S(2)}) collective-permute-start(bf16[512,1024]{1,0:T(8,128)(2,1)} %get-tuple-element.86), channel_id=1, source_target_pairs={{0,128},{128,0},{1,129},{129,1},{2,130},{130,2},{3,131},{131,3},{4... | collective-permute-start | bytes 3145736 | tf_op jit(solution)/shard_map/ppermute | solution.py:18
  214.5 1.3 collective-permute-start.8
  215.9 4.3 %broadcast_select_fusion.2 = (bf16[1024,896]{1,0:T(8,128)(2,1)}, bf16[1024,896]{1,0:T(8,128)(2,1)}) fusion(bf16[1024,896]{1,0:T(8,128)(2,1)S(1)} %bitcast.148, bf16[1024,896]{1,0:T(8,128)(2,1)} %collective-permute-done.5, pred[]{:T(512)S(6)} %eq.3, bf16[1024,896]{1,0:T(8,128)(2,1)S(1)} %bitcast.150, bf16[1024,896]{1,0:T(8,128)(2,1)} %collective-permute-done.4), kind=kLoop, calls=%fused_computation.76 | loop fusion | flops 1835008 | bytes 11010049 | tf_op jit(solution)/shard_map/jit(_where)/select_n | solution.py:164
  220.2 9.8 %all-to-all-done.7 = bf16[8,64,896]{2,1,0:T(8,128)(2,1)} async-done(((bf16[8,64,896]{2,1,0:T(8,128)(2,1)}), bf16[8,64,896]{2,1,0:T(8,128)(2,1)}, u32[]{:S(2)}, u32[]{:S(2)}) %all-to-all-start.7) | async-done | bytes 917536 | tf_op jit(solution)/shard_map/all_to_all | solution.py:26
  230.0 7.1 %collective-permute-start.15 = (bf16[512,896]{1,0:T(8,128)(2,1)}, bf16[512,896]{1,0:T(8,128)(2,1)}, u32[]{:S(2)}, u32[]{:S(2)}) collective-permute-start(bf16[512,896]{1,0:T(8,128)(2,1)} %bitcast.30), channel_id=1, source_target_pairs={{128,0},{129,1},{130,2},{131,3},{132,4},{133,5},{134,6},{135,7},{1... | collective-permute-start | bytes 2752520 | tf_op jit(solution)/shard_map/ppermute | solution.py:124
  237.1 3.1 %fusion.9 = (bf16[512,896]{1,0:T(8,128)(2,1)S(1)}, bf16[512,896]{1,0:T(8,128)(2,1)S(1)}) fusion(bf16[512,896]{1,0:T(8,128)(2,1)} %bitcast.30, bf16[2,1,512,896]{3,2,1,0:T(8,128)(2,1)} %bitcast.154, bf16[2,1,512,896]{3,2,0,1:T(8,128)(2,1)} %all-gather.6.cloned.1.call-done), kind=kLoop, calls=%fused_computation.29 | loop fusion | flops 7340032 | bytes 4587520 | tf_op jit(solution)/shard_map/convert_element_type | solution.py:38
  240.2 1.3 fusion.88
  241.5 0.8 copy-done.14
  242.3 2.3 add_convert_fusion
  244.6 4.4 %all-to-all-start.8 = ((bf16[16,32,1024]{2,1,0:T(8,128)(2,1)}), bf16[16,32,1024]{2,1,0:T(8,128)(2,1)S(1)}, u32[]{:S(2)}, u32[]{:S(2)}) async-start(bf16[16,32,1024]{2,1,0:T(8,128)(2,1)} %bitcast.157), calls=%async_computation.8 | async-start | bytes 2097152 | tf_op jit(solution)/shard_map/all_to_all | solution.py:26
  249.0 1.4 broadcast_select_fusion.10
  250.8 1.1 copy-done.18
  252.0 1.0 fusion.38
  253.6 3.6 %convert_bitcast_fusion = bf16[1,1024,896]{2,1,0:T(8,128)(2,1)} fusion(bf16[1024,1024]{1,0:T(8,128)(2,1)S(1)} %bitcast.180, bf16[512,896]{1,0:T(8,128)(2,1)S(1)} %get-tuple-element.79, bf16[512,896]{1,0:T(8,128)(2,1)S(1)} %broadcast_select_fusion.10), kind=kOutput, calls=%fused_computation.70 | convolution fusion | flops 1883635712 | bytes 5767168 | tf_op jit(solution)/shard_map/dot_general | solution.py:14
  257.2 3.6 %convert_bitcast_fusion.1 = bf16[1,1024,896]{2,1,0:T(8,128)(2,1)} fusion(bf16[1024,1024]{1,0:T(8,128)(2,1)S(1)} %bitcast.181, bf16[512,896]{1,0:T(8,128)(2,1)S(1)} %get-tuple-element.80, bf16[512,896]{1,0:T(8,128)(2,1)S(1)} %broadcast_select_fusion.12), kind=kOutput, calls=%fused_computation.71 | convolution fusion | flops 1883635712 | bytes 5767168 | tf_op jit(solution)/shard_map/dot_general | solution.py:14
  260.9 5.4 %all-to-all-done.8 = bf16[16,32,1024]{2,1,0:T(8,128)(2,1)S(1)} async-done(((bf16[16,32,1024]{2,1,0:T(8,128)(2,1)}), bf16[16,32,1024]{2,1,0:T(8,128)(2,1)S(1)}, u32[]{:S(2)}, u32[]{:S(2)}) %all-to-all-start.8) | async-done | bytes 1048608 | tf_op jit(solution)/shard_map/all_to_all | solution.py:26
  266.9 2.4 collective-permute-start.11
  270.1 1.5 fusion.51
  272.4 3.5 %all-to-all-start.9 = ((f32[16,2,1024]{2,1,0:T(2,128)}), f32[16,2,1024]{2,1,0:T(2,128)S(1)}, u32[]{:S(2)}, u32[]{:S(2)}) async-start(f32[16,2,1024]{2,1,0:T(2,128)} %broadcast_in_dim.25), calls=%async_computation.9 | async-start | bytes 262144 | tf_op jit(solution)/shard_map/all_to_all | solution.py:26
  275.9 0.9 collective-permute-start.12
  276.9 4.8 %fusion.56 = bf16[896,1024]{1,0:T(8,128)(2,1)} fusion(bf16[512,1024]{1,0:T(8,128)(2,1)} %collective-permute-done.7, bf16[512,1024]{1,0:T(8,128)(2,1)S(1)} %copy-done.16, bf16[512,896]{1,0:T(8,128)(2,1)S(1)} %fusion.50, bf16[512,896]{1,0:T(8,128)(2,1)} %fusion.51), kind=kOutput, calls=%fused_computation.82 | convolution fusion | flops 1887830016 | bytes 5767168 | tf_op jit(solution)/shard_map/dot_general | solution.py:14
  282.5 2.3 collective-permute-start.13
  (103 shorter events, 10.0 us)
Async XLA Ops:
  7.2 8.1 %copy-start.20 = (bf16[64,1024]{1,0:T(8,128)(2,1)S(1)}, bf16[64,1024]{1,0:T(8,128)(2,1)}, u32[]{:S(2)}) copy-start(bf16[64,1024]{1,0:T(8,128)(2,1)} %param.15) | copy-start | bytes 393220
  7.2 69.0 %all-gather.4.cloned.1.call-start = ((), (), s32[]{:S(2)}) async-start(), calls=%async_computation.10 | async-start | bytes 2064384 | tf_op jit(solution)/shard_map/all_gather | solution.py:71
  8.3 4.4 %collective-permute-start.1 = (bf16[2,2,32,896]{3,2,1,0:T(8,128)(2,1)S(1)}, bf16[2,2,32,896]{3,2,1,0:T(8,128)(2,1)S(1)}, u32[]{:S(2)}, u32[]{:S(2)}) collective-permute-start(bf16[2,2,32,896]{3,2,1,0:T(8,128)(2,1)S(1)} %fusion.65), channel_id=1, source_target_pairs={{0,128},{128,0},{1,129},{129,1},{2,130},{130,2},{3,131},{131,3},{4... | collective-permute-start | bytes 688136 | tf_op jit(solution)/shard_map/ppermute | solution.py:18
  12.8 8.6 %collective-permute-start.2 = (bf16[896,1024]{1,0:T(8,128)(2,1)}, bf16[896,1024]{1,0:T(8,128)(2,1)}, u32[]{:S(2)}, u32[]{:S(2)}) collective-permute-start(bf16[896,1024]{1,0:T(8,128)(2,1)} %bitcast.145), channel_id=1, source_target_pairs={{0,128},{128,0},{1,129},{129,1},{2,130},{130,2},{3,131},{131,3},{4... | collective-permute-start | bytes 5505032 | tf_op jit(solution)/shard_map/ppermute | solution.py:18
  15.2 6.2 %copy-start = (bf16[1,896,1024]{2,1,0:T(8,128)(2,1)S(1)}, bf16[1,896,1024]{2,1,0:T(8,128)(2,1)}, u32[]{:S(2)}) copy-start(bf16[1,896,1024]{2,1,0:T(8,128)(2,1)} %param.14) | copy-start | bytes 5505028
  16.4 21.8 %all-to-all-start = ((bf16[16,32,1024]{2,1,0:T(8,128)(2,1)}), bf16[16,32,1024]{2,1,0:T(8,128)(2,1)S(1)}, u32[]{:S(2)}, u32[]{:S(2)}) async-start(bf16[16,32,1024]{2,1,0:T(8,128)(2,1)} %broadcast_in_dim.20), calls=%async_computation | async-start | bytes 2097152 | tf_op jit(solution)/shard_map/all_to_all | solution.py:26
  41.9 33.0 %all-to-all-start.1 = ((bf16[8,64,896]{2,1,0:T(8,128)(2,1)}), bf16[8,64,896]{2,1,0:T(8,128)(2,1)}, u32[]{:S(2)}, u32[]{:S(2)}) async-start(bf16[8,64,896]{2,1,0:T(8,128)(2,1)} %bitcast.160), calls=%async_computation.1 | async-start | bytes 1835008 | tf_op jit(solution)/shard_map/all_to_all | solution.py:26
  50.0 31.4 %collective-permute-start.5 = (bf16[1024,896]{1,0:T(8,128)(2,1)}, bf16[1024,896]{1,0:T(8,128)(2,1)}, u32[]{:S(2)}, u32[]{:S(2)}) collective-permute-start(bf16[1024,896]{1,0:T(8,128)(2,1)} %bitcast.147), channel_id=1, source_target_pairs={{0,128},{128,0},{1,129},{129,1},{2,130},{130,2},{3,131},{131,3},{4... | collective-permute-start | bytes 5505032 | tf_op jit(solution)/shard_map/ppermute | solution.py:18
  52.2 32.4 %collective-permute-start.4 = (bf16[1024,896]{1,0:T(8,128)(2,1)}, bf16[1024,896]{1,0:T(8,128)(2,1)}, u32[]{:S(2)}, u32[]{:S(2)}) collective-permute-start(bf16[1024,896]{1,0:T(8,128)(2,1)} %bitcast.149), channel_id=1, source_target_pairs={{0,128},{128,0},{1,129},{129,1},{2,130},{130,2},{3,131},{131,3},{4... | collective-permute-start | bytes 5505032 | tf_op jit(solution)/shard_map/ppermute | solution.py:18
  77.3 30.6 %all-to-all-start.2 = ((bf16[8,64,896]{2,1,0:T(8,128)(2,1)}), bf16[8,64,896]{2,1,0:T(8,128)(2,1)}, u32[]{:S(2)}, u32[]{:S(2)}) async-start(bf16[8,64,896]{2,1,0:T(8,128)(2,1)} %broadcast_in_dim.21), calls=%async_computation.2 | async-start | bytes 1835008 | tf_op jit(solution)/shard_map/all_to_all | solution.py:26
  81.5 3.1 %copy-start.2 = (bf16[1,1024,896]{2,1,0:T(8,128)(2,1)S(1)}, bf16[1,1024,896]{2,1,0:T(8,128)(2,1)}, u32[]{:S(2)}) copy-start(bf16[1,1024,896]{2,1,0:T(8,128)(2,1)} %param.12) | copy-start | bytes 5505028
  107.9 2.9 copy-start.12
  110.7 1.3 copy-start.8
  110.7 1.3 copy-start.6
  110.7 2.2 copy-start.13
  115.1 6.9 %copy-start.21 = (f32[1,1024]{1,0:T(1,128)S(1)}, f32[1,1024]{1,0:T(1,128)}, u32[]{:S(2)}) copy-start(f32[1,1024]{1,0:T(1,128)} %param.9) | copy-start | bytes 12292
  115.1 7.8 %copy-start.19 = (bf16[1,64,1024]{2,1,0:T(8,128)(2,1)S(1)}, bf16[1,64,1024]{2,1,0:T(8,128)(2,1)}, u32[]{:S(2)}) copy-start(bf16[1,64,1024]{2,1,0:T(8,128)(2,1)} %param.8) | copy-start | bytes 393220
  115.1 22.4 %all-to-all-start.3 = ((bf16[16,32,1024]{2,1,0:T(8,128)(2,1)}), bf16[16,32,1024]{2,1,0:T(8,128)(2,1)}, u32[]{:S(2)}, u32[]{:S(2)}) async-start(bf16[16,32,1024]{2,1,0:T(8,128)(2,1)} %bitcast.158), calls=%async_computation.3 | async-start | bytes 2097152 | tf_op jit(solution)/shard_map/all_to_all | solution.py:26
  121.3 52.4 %all-gather.6.cloned.1.call-start = ((), (), s32[]{:S(2)}) async-start(), calls=%async_computation.11 | async-start | bytes 2064384 | tf_op jit(solution)/shard_map/all_gather | solution.py:71
  122.1 1.7 collective-permute-start.3
  122.9 16.1 %collective-permute-start = (bf16[32,1024]{1,0:T(8,128)(2,1)S(1)}, bf16[32,1024]{1,0:T(8,128)(2,1)S(1)}, u32[]{:S(2)}, u32[]{:S(2)}) collective-permute-start(bf16[32,1024]{1,0:T(8,128)(2,1)S(1)} %select_bitcast_fusion.1), channel_id=1, source_target_pairs={{0,128},{128,0},{1,129},{129,1},{2,130},{130,2},{3,131},{131,3},{4... | collective-permute-start | bytes 196616 | tf_op jit(solution)/shard_map/ppermute | solution.py:18
  151.2 18.6 %all-to-all-start.5 = ((bf16[16,32,1024]{2,1,0:T(8,128)(2,1)}), bf16[16,32,1024]{2,1,0:T(8,128)(2,1)}, u32[]{:S(2)}, u32[]{:S(2)}) async-start(bf16[16,32,1024]{2,1,0:T(8,128)(2,1)} %broadcast_in_dim.23), calls=%async_computation.5 | async-start | bytes 2097152 | tf_op jit(solution)/shard_map/all_to_all | solution.py:26
  173.7 5.5 %copy-start.5 = (bf16[2,1,512,896]{3,2,0,1:T(8,128)(2,1)S(1)}, bf16[2,1,512,896]{3,2,0,1:T(8,128)(2,1)}, u32[]{:S(2)}) copy-start(bf16[2,1,512,896]{3,2,0,1:T(8,128)(2,1)} %all-gather.4.cloned.1.call-done) | copy-start | bytes 5505028
  173.7 27.0 %all-to-all-start.6 = ((bf16[8,64,896]{2,1,0:T(8,128)(2,1)}), bf16[8,64,896]{2,1,0:T(8,128)(2,1)}, u32[]{:S(2)}, u32[]{:S(2)}) async-start(bf16[8,64,896]{2,1,0:T(8,128)(2,1)} %bitcast.159), calls=%async_computation.6 | async-start | bytes 1835008 | tf_op jit(solution)/shard_map/all_to_all | solution.py:26
  178.1 66.5 %all-gather.8.cloned.1.call-start = ((), (), s32[]{:S(2)}) async-start(), calls=%async_computation.12 | async-start | bytes 2228224 | tf_op jit(solution)/shard_map/all_gather | solution.py:155
  182.9 54.2 %collective-permute-start.6 = (bf16[2,512,896]{2,1,0:T(8,128)(2,1)}, bf16[2,512,896]{2,1,0:T(8,128)(2,1)S(1)}, u32[]{:S(2)}, u32[]{:S(2)}) collective-permute-start(bf16[2,512,896]{2,1,0:T(8,128)(2,1)} %get-tuple-element.78), channel_id=1, source_target_pairs={{0,128},{128,0},{1,129},{129,1},{2,130},{130,2},{3,131},{131,3},{4... | collective-permute-start | bytes 5505032 | tf_op jit(solution)/shard_map/ppermute | solution.py:18
  203.1 26.9 %all-to-all-start.7 = ((bf16[8,64,896]{2,1,0:T(8,128)(2,1)}), bf16[8,64,896]{2,1,0:T(8,128)(2,1)}, u32[]{:S(2)}, u32[]{:S(2)}) async-start(bf16[8,64,896]{2,1,0:T(8,128)(2,1)} %broadcast_in_dim.24), calls=%async_computation.7 | async-start | bytes 1835008 | tf_op jit(solution)/shard_map/all_to_all | solution.py:26
  207.3 8.6 %copy-start.1 = (bf16[1,1024,896]{2,1,0:T(8,128)(2,1)S(1)}, bf16[1,1024,896]{2,1,0:T(8,128)(2,1)}, u32[]{:S(2)}) copy-start(bf16[1,1024,896]{2,1,0:T(8,128)(2,1)} %param.13) | copy-start | bytes 5505028
  207.3 8.5 %copy-start.3 = (bf16[1,1024,896]{2,1,0:T(8,128)(2,1)S(1)}, bf16[1,1024,896]{2,1,0:T(8,128)(2,1)}, u32[]{:S(2)}) copy-start(bf16[1,1024,896]{2,1,0:T(8,128)(2,1)} %param.12) | copy-start | bytes 5505028
  210.2 26.9 %collective-permute-start.7 = (bf16[512,1024]{1,0:T(8,128)(2,1)}, bf16[512,1024]{1,0:T(8,128)(2,1)}, u32[]{:S(2)}, u32[]{:S(2)}) collective-permute-start(bf16[512,1024]{1,0:T(8,128)(2,1)} %get-tuple-element.86), channel_id=1, source_target_pairs={{0,128},{128,0},{1,129},{129,1},{2,130},{130,2},{3,131},{131,3},{4... | collective-permute-start | bytes 3145736 | tf_op jit(solution)/shard_map/ppermute | solution.py:18
  214.5 22.6 %collective-permute-start.8 = (bf16[512,896]{1,0:T(8,128)(2,1)}, bf16[512,896]{1,0:T(8,128)(2,1)S(1)}, u32[]{:S(2)}, u32[]{:S(2)}) collective-permute-start(bf16[512,896]{1,0:T(8,128)(2,1)} %bitcast.14), channel_id=1, source_target_pairs={{0,128},{1,129},{2,130},{3,131},{4,132},{5,133},{6,134},{7,135},{8... | collective-permute-start | bytes 2752520 | tf_op jit(solution)/shard_map/ppermute | solution.py:124
  230.0 20.8 %collective-permute-start.15 = (bf16[512,896]{1,0:T(8,128)(2,1)}, bf16[512,896]{1,0:T(8,128)(2,1)}, u32[]{:S(2)}, u32[]{:S(2)}) collective-permute-start(bf16[512,896]{1,0:T(8,128)(2,1)} %bitcast.30), channel_id=1, source_target_pairs={{128,0},{129,1},{130,2},{131,3},{132,4},{133,5},{134,6},{135,7},{1... | collective-permute-start | bytes 2752520 | tf_op jit(solution)/shard_map/ppermute | solution.py:124
  237.1 3.1 %copy-start.17 = (bf16[512,896]{1,0:T(8,128)(2,1)}, bf16[512,896]{1,0:T(8,128)(2,1)S(1)}, u32[]{:S(2)}) copy-start(bf16[512,896]{1,0:T(8,128)(2,1)S(1)} %collective-permute-done.8) | copy-start | bytes 2752516
  237.1 3.1 %copy-start.15 = (bf16[1024,896]{1,0:T(8,128)(2,1)S(1)}, bf16[1024,896]{1,0:T(8,128)(2,1)}, u32[]{:S(2)}) copy-start(bf16[1024,896]{1,0:T(8,128)(2,1)} %get-tuple-element.99) | copy-start | bytes 5505028
  240.2 1.3 copy-start.11
  240.2 1.3 copy-start.9
  240.2 2.2 copy-start.14
  244.6 21.7 %all-to-all-start.8 = ((bf16[16,32,1024]{2,1,0:T(8,128)(2,1)}), bf16[16,32,1024]{2,1,0:T(8,128)(2,1)S(1)}, u32[]{:S(2)}, u32[]{:S(2)}) async-start(bf16[16,32,1024]{2,1,0:T(8,128)(2,1)} %bitcast.157), calls=%async_computation.8 | async-start | bytes 2097152 | tf_op jit(solution)/shard_map/all_to_all | solution.py:26
  249.0 1.5 copy-start.7
  249.0 1.7 copy-start.10
  250.7 1.2 copy-start.18
  252.0 1.6 copy-start.22
  266.4 3.7 %copy-start.4 = (bf16[2,512,896]{2,1,0:T(8,128)(2,1)S(1)}, bf16[2,512,896]{2,1,0:T(8,128)(2,1)}, u32[]{:S(2)}) copy-start(bf16[2,512,896]{2,1,0:T(8,128)(2,1)} %get-tuple-element.59) | copy-start | bytes 5505028
  266.6 9.3 %collective-permute-start.10 = (f32[32]{0:T(128)S(1)}, f32[32]{0:T(128)S(1)}, u32[]{:S(2)}, u32[]{:S(2)}) collective-permute-start(f32[32]{0:T(128)S(1)} %get-tuple-element.70), channel_id=1, source_target_pairs={{0,32},{16,48},{32,0},{48,16},{64,96},{80,112},{96,64},{112,80},{1... | collective-permute-start | bytes 392 | tf_op jit(solution)/shard_map/ppermute | solution.py:179
  266.9 9.0 %collective-permute-start.11 = (f32[32]{0:T(128)S(1)}, f32[32]{0:T(128)S(1)}, u32[]{:S(2)}, u32[]{:S(2)}) collective-permute-start(f32[32]{0:T(128)S(1)} %get-tuple-element.70), channel_id=1, source_target_pairs={{0,48},{16,32},{32,16},{48,0},{64,112},{80,96},{96,80},{112,64},{1... | collective-permute-start | bytes 392 | tf_op jit(solution)/shard_map/ppermute | solution.py:179
  269.3 6.6 %collective-permute-start.9 = (f32[32]{0:T(128)S(1)}, f32[32]{0:T(128)S(1)}, u32[]{:S(2)}, u32[]{:S(2)}) collective-permute-start(f32[32]{0:T(128)S(1)} %get-tuple-element.70), channel_id=1, source_target_pairs={{0,16},{16,0},{32,48},{48,32},{64,80},{80,64},{96,112},{112,96},{1... | collective-permute-start | bytes 392 | tf_op jit(solution)/shard_map/ppermute | solution.py:179
  270.1 6.7 %copy-start.16 = (bf16[512,1024]{1,0:T(8,128)(2,1)S(1)}, bf16[512,1024]{1,0:T(8,128)(2,1)}, u32[]{:S(2)}) copy-start(bf16[512,1024]{1,0:T(8,128)(2,1)} %get-tuple-element.61) | copy-start | bytes 3145732
  272.4 12.4 %all-to-all-start.9 = ((f32[16,2,1024]{2,1,0:T(2,128)}), f32[16,2,1024]{2,1,0:T(2,128)S(1)}, u32[]{:S(2)}, u32[]{:S(2)}) async-start(f32[16,2,1024]{2,1,0:T(2,128)} %broadcast_in_dim.25), calls=%async_computation.9 | async-start | bytes 262144 | tf_op jit(solution)/shard_map/all_to_all | solution.py:26
  275.9 6.4 %collective-permute-start.12 = (f32[32]{0:T(128)S(1)}, f32[32]{0:T(128)S(1)}, u32[]{:S(2)}, u32[]{:S(2)}) collective-permute-start(f32[32]{0:T(128)S(1)} %add_add_fusion), channel_id=1, source_target_pairs={{0,64},{16,80},{32,96},{48,112},{64,0},{80,16},{96,32},{112,48},{1... | collective-permute-start | bytes 392 | tf_op jit(solution)/shard_map/ppermute | solution.py:181
  282.5 3.2 %collective-permute-start.13 = (bf16[32,1024]{1,0:T(8,128)(2,1)S(1)}, bf16[32,1024]{1,0:T(8,128)(2,1)S(1)}, u32[]{:S(2)}, u32[]{:S(2)}) collective-permute-start(bf16[32,1024]{1,0:T(8,128)(2,1)S(1)} %get-tuple-element.90), channel_id=1, source_target_pairs={{0,128},{128,0},{1,129},{129,1},{2,130},{130,2},{3,131},{131,3},{4... | collective-permute-start | bytes 196616 | tf_op jit(solution)/shard_map/ppermute | solution.py:18
  284.9 1.5 collective-permute-start.14
Sparse Core Ops, SparseCore 0:
  15.3 37.7 all-gather.3
  123.9 32.9 all-gather.5
  182.0 50.7 all-gather.7

commit v2 on v1

--- a/solution.py
+++ b/solution.py
@@ -90,8 +90,8 @@
     def all_units(grad_local):
         return spread(grad_local, "row").reshape(cols * half, units)
 
-    def normed_grads(partial):
-        pieces = exchange(partial.reshape(cols, half, features), "col")
+    def normed_grads(partial, beside=()):
+        pieces = after(exchange(partial.reshape(cols, half, features), "col"), beside)
         return jnp.sum(pieces.astype(f32), axis=0)
 
     def inner(normed_grad, hidden, gain):
@@ -140,7 +140,10 @@
     gate_grad1, up_grad1 = unit_grads(hidden_grad1, saved1[:, 0])
     partial = into_features(gate_grad1, up_grad1, gates1, ups1)
     saved0 = gather_saved(after(saved0, gate_grad1))
-    normed_grad1 = normed_grads(partial)
+    weights = after((gate_own, gate_swapped, up_own, up_swapped), partial)
+    gates0 = lax.optimization_barrier(jnp.where(first, weights[0], weights[1]))
+    ups0 = lax.optimization_barrier(jnp.where(first, weights[2], weights[3]))
+    normed_grad1 = normed_grads(partial, (gates0, ups0))
     sums = over_rows(jnp.concatenate([squares, inner(normed_grad1, hid1, gain1)]))
     inv = lax.rsqrt(sums[: 3 * half] / D + EPSILON)
     inv1, inv0 = by_layer(inv[:half], inv[2 * half :])
@@ -159,10 +162,9 @@
     saved_own, saved_theirs = both_halves(saved1[:, 0], saved0[:, 0], cot_all0)
     cot_own, cot_theirs = both_halves(cot_all1, cot_all0, cot_all0)
     grad_early = handed(after(hidden_grad1, cot_all0), 0, 1)
-    weights = lax.optimization_barrier((gate_own, gate_swapped, up_own, up_swapped, grad_local))
-    gates0 = lax.optimization_barrier(jnp.where(first, weights[0], weights[1]))
-    ups0 = lax.optimization_barrier(jnp.where(first, weights[2], weights[3]))
-    ready = (saved_theirs, cot_theirs, grad_early, gates0, ups0)
+    acts = jnp.concatenate([activation(saved_own), activation(saved_theirs)], axis=0)
+    grad_down = dot(acts, jnp.concatenate([cot_own, cot_theirs], axis=0), ((0,), (0,))).astype(bf16)
+    ready = (saved_theirs, grad_down, grad_early)
     gate_grad0, up_grad0 = unit_grads(after(hidden_grad0, ready), saved0[:, 0])
     partial = after(into_features(gate_grad0, up_grad0, gates0, ups0), normed)
     normed_grad0 = normed_grads(partial)
@@ -172,9 +174,6 @@
     gate_own, up_own = jnp.where(first, gate0, gate1), jnp.where(first, up0, up1)
     gate_grads = jnp.concatenate([gate_own, gate_theirs], axis=0)
     up_grads = jnp.concatenate([up_own, up_theirs], axis=0)
-    saved_own, saved_late, cot_own, cot_theirs = after((saved_own, saved_theirs, cot_own, cot_theirs), normed_grad0)
-    acts = jnp.concatenate([activation(saved_own), activation(saved_late)], axis=0)
-    grad_down = dot(acts, jnp.concatenate([cot_own, cot_theirs], axis=0), ((0,), (0,))).astype(bf16)
     cross = inner(normed_grad0, hid0, gain0)
     others = [lax.ppermute(cross, "row", [(i, i ^ bits) for i in range(rows)]) for bits in (1, 2, 3)]
     cross = cross + others[0] + others[1] + others[2]
@@ -189,7 +188,7 @@
     gain1_part = gain_part(normed_grad1, hid1, inv1)
     gain0_part = gain_part(normed_grad0, hid0, inv0)
     gain_parts = jnp.stack([jnp.where(first, gain0_part, gain1_part), jnp.where(first, gain1_part, gain0_part)])
-    gain_parts = jnp.sum(after(spread(gain_parts, "col"), grad_down), axis=0)
+    gain_parts = jnp.sum(spread(gain_parts, "col"), axis=0)
     gain_total = gain_parts[0] + swap(gain_parts[1])
     own = jnp.where(first, result0, result1)
     other = swap(jnp.where(first, result1, result0))

time: 295 us -> 296 us (level)
  starting transfers between devices: 75.4 us -> 79 us
    ppermute x10, starting transfers between devices: 18.3 us -> 21.7 us  [swap(): return lax.ppermute(block, 'section', [(0, 1), (1, 0)])]
  transfers between devices with their start and end apart: 28 -> 28, of which waited for: 12 -> 15; matrix products, arithmetic and copies ran while one was open for 22% -> 21% of each run, Pallas kernels for 0% -> 0%
where the time goes in v2:
time: 296 us; the launch traced here: 294 us
  waiting for transfers between devices  118 us (40%)
  starting transfers between devices  79 us (27%)
  other arithmetic  40 us (14%)
  matrix products  25.5 us (9%)
  between operations  14.2 us (5%)
  blocking collectives  8.98 us (3%)
  local copies, waits for them, and re-layouts  8.83 us (3%)
    all_to_all x9, waiting for transfers between devices, exchange(): return lax.all_to_all(blocks, axis, 0, 0)  113 us
    all_to_all x9, starting transfers between devices, exchange(): return lax.all_to_all(blocks, axis, 0, 0)  44.6 us
    dot_general x9, matrix products, dot(): lax.dot_general(left, right, (dims, ((), ())), preferred_element_type=f32)  25.5 us
    ppermute x10, starting transfers between devices, swap(): return lax.ppermute(block, 'section', [(0, 1), (1, 0)])  21.7 us
    all_to_all x1, blocking collectives, exchange(): return lax.all_to_all(blocks, axis, 0, 0)  8.98 us
    ppermute x2, starting transfers between devices, handed(): return lax.ppermute(block, 'section', [(source, target)])  8.39 us
  transfers between devices with their start and end apart: 28, of which 15 were waited for; matrix products, arithmetic and copies ran while one was open for 21% of the time, Pallas kernels for 0%

profile of v2, /device:TPU:1, one launch (start us, length us, event | category | flops | bytes accessed | tf_op | source)
XLA Modules:
  0.0 294.3 jit_solution(16530431565313417551)
XLA Ops:
  7.2 1.1 fusion.61
  8.3 3.3 %collective-permute-start.1 = (bf16[2,2,32,896]{3,2,1,0:T(8,128)(2,1)S(1)}, bf16[2,2,32,896]{3,2,1,0:T(8,128)(2,1)S(1)}, u32[]{:S(2)}, u32[]{:S(2)}) collective-permute-start(bf16[2,2,32,896]{3,2,1,0:T(8,128)(2,1)S(1)} %fusion.61), channel_id=1, source_target_pairs={{0,128},{128,0},{1,129},{129,1},{2,130},{130,2},{3,131},{131,3},{4... | collective-permute-start | bytes 688136 | tf_op jit(solution)/shard_map/ppermute | solution.py:18
  11.7 1.1 collective-permute-done.1
  13.2 2.0 broadcast_select_fusion.13
  15.3 1.1 broadcast_in_dim.20
  16.4 5.0 %all-to-all-start = ((bf16[16,32,1024]{2,1,0:T(8,128)(2,1)}), bf16[16,32,1024]{2,1,0:T(8,128)(2,1)S(1)}, u32[]{:S(2)}, u32[]{:S(2)}) async-start(bf16[16,32,1024]{2,1,0:T(8,128)(2,1)} %broadcast_in_dim.20), calls=%async_computation | async-start | bytes 2097152 | tf_op jit(solution)/shard_map/all_to_all | solution.py:26
  21.4 1.4 broadcast_select_fusion.7
  22.8 15.3 %all-to-all-done = bf16[16,32,1024]{2,1,0:T(8,128)(2,1)S(1)} async-done(((bf16[16,32,1024]{2,1,0:T(8,128)(2,1)}), bf16[16,32,1024]{2,1,0:T(8,128)(2,1)S(1)}, u32[]{:S(2)}, u32[]{:S(2)}) %all-to-all-start) | async-done | bytes 1048608 | tf_op jit(solution)/shard_map/all_to_all | solution.py:26
  38.1 3.7 %convolution_convert_fusion.1 = bf16[512,896]{1,0:T(8,128)(2,1)} fusion(bf16[512,1024]{1,0:T(8,128)(2,1)S(1)} %bitcast.157, bf16[896,1024]{1,0:T(8,128)(2,1)} %broadcast_select_fusion.7), kind=kOutput, calls=%fused_computation.80 | convolution fusion | flops 939982848 | bytes 3801088 | tf_op jit(solution)/shard_map/dot_general | solution.py:14
  41.9 8.2 %all-to-all-start.1 = ((bf16[8,64,896]{2,1,0:T(8,128)(2,1)}), bf16[8,64,896]{2,1,0:T(8,128)(2,1)}, u32[]{:S(2)}, u32[]{:S(2)}) async-start(bf16[8,64,896]{2,1,0:T(8,128)(2,1)} %bitcast.162), calls=%async_computation.1 | async-start | bytes 1835008 | tf_op jit(solution)/shard_map/all_to_all | solution.py:26
  50.0 2.1 collective-permute-start.5
  52.3 22.6 %all-to-all-done.1 = bf16[8,64,896]{2,1,0:T(8,128)(2,1)} async-done(((bf16[8,64,896]{2,1,0:T(8,128)(2,1)}), bf16[8,64,896]{2,1,0:T(8,128)(2,1)}, u32[]{:S(2)}, u32[]{:S(2)}) %all-to-all-start.1) | async-done | bytes 917536 | tf_op jit(solution)/shard_map/all_to_all | solution.py:26
  74.9 1.3 reduce_sum.108
  76.2 1.0 broadcast_in_dim.21
  77.3 4.2 %all-to-all-start.2 = ((bf16[8,64,896]{2,1,0:T(8,128)(2,1)}), bf16[8,64,896]{2,1,0:T(8,128)(2,1)}, u32[]{:S(2)}, u32[]{:S(2)}) async-start(bf16[8,64,896]{2,1,0:T(8,128)(2,1)} %broadcast_in_dim.21), calls=%async_computation.2 | async-start | bytes 1835008 | tf_op jit(solution)/shard_map/all_to_all | solution.py:26
  81.5 3.1 %broadcast_select_fusion.4 = bf16[1024,896]{1,0:T(8,128)(2,1)} fusion(bf16[1024,896]{1,0:T(8,128)(2,1)} %collective-permute-done.5, pred[]{:T(512)S(6)} %eq.3, bf16[1,1024,896]{2,1,0:T(8,128)(2,1)} %param.13), kind=kLoop, calls=%fused_computation.74 | loop fusion | flops 917504 | bytes 5505025 | tf_op jit(solution)/shard_map/jit(_where)/select_n | solution.py:134
  84.6 1.4 broadcast_select_fusion.5
  86.0 21.9 %all-to-all-done.2 = bf16[8,64,896]{2,1,0:T(8,128)(2,1)} async-done(((bf16[8,64,896]{2,1,0:T(8,128)(2,1)}), bf16[8,64,896]{2,1,0:T(8,128)(2,1)}, u32[]{:S(2)}, u32[]{:S(2)}) %all-to-all-start.2) | async-done | bytes 917536 | tf_op jit(solution)/shard_map/all_to_all | solution.py:26
  107.9 2.8 fusion.6
  110.7 1.3 fusion.83
  112.9 2.2 add_convert_fusion.1
  115.1 6.2 %all-to-all-start.3 = ((bf16[16,32,1024]{2,1,0:T(8,128)(2,1)}), bf16[16,32,1024]{2,1,0:T(8,128)(2,1)}, u32[]{:S(2)}, u32[]{:S(2)}) async-start(bf16[16,32,1024]{2,1,0:T(8,128)(2,1)} %bitcast.159), calls=%async_computation.3 | async-start | bytes 2097152 | tf_op jit(solution)/shard_map/all_to_all | solution.py:26
  121.4 0.9 collective-permute-start.3
  123.1 4.3 %broadcast_select_fusion.2 = (bf16[1024,896]{1,0:T(8,128)(2,1)}, bf16[1024,896]{1,0:T(8,128)(2,1)}) fusion(bf16[1024,896]{1,0:T(8,128)(2,1)} %bitcast.150, bf16[1024,896]{1,0:T(8,128)(2,1)} %collective-permute-done.5, pred[]{:T(512)S(6)} %eq.3, bf16[1024,896]{1,0:T(8,128)(2,1)} %bitcast.152, bf16[1024,896]{1,0:T(8,128)(2,1)} %collective-permute-done.4), kind=kLoop, calls=%fused_computation.72 | loop fusion | flops 1835008 | bytes 11010049 | tf_op jit(solution)/shard_map/jit(_where)/select_n | solution.py:145
  127.3 10.2 %all-to-all-done.3 = bf16[16,32,1024]{2,1,0:T(8,128)(2,1)} async-done(((bf16[16,32,1024]{2,1,0:T(8,128)(2,1)}), bf16[16,32,1024]{2,1,0:T(8,128)(2,1)}, u32[]{:S(2)}, u32[]{:S(2)}) %all-to-all-start.3) | async-done | bytes 1048608 | tf_op jit(solution)/shard_map/all_to_all | solution.py:26
  137.6 1.4 convert_reduce_fusion.1
  140.0 9.0 %all_to_all.50 = f32[8,1,128]{2,1,0:T(1,128)S(1)} all-to-all(f32[8,1,128]{2,1,0:T(1,128)S(1)} %broadcast_in_dim.22), channel_id=1, replica_groups=mesh['section'=2,'row'=8,'col'=16] {'row'}, dimensions={0} | all-to-all | bytes 8192 | tf_op jit(solution)/shard_map/all_to_all | solution.py:26
  149.1 1.0 fusion.66
  150.1 1.1 broadcast_in_dim.23
  151.2 4.6 %all-to-all-start.5 = ((bf16[16,32,1024]{2,1,0:T(8,128)(2,1)}), bf16[16,32,1024]{2,1,0:T(8,128)(2,1)}, u32[]{:S(2)}, u32[]{:S(2)}) async-start(bf16[16,32,1024]{2,1,0:T(8,128)(2,1)} %broadcast_in_dim.23), calls=%async_computation.5 | async-start | bytes 2097152 | tf_op jit(solution)/shard_map/all_to_all | solution.py:26
  155.7 2.9 broadcast_select_fusion.6
  158.7 11.0 %all-to-all-done.5 = bf16[16,32,1024]{2,1,0:T(8,128)(2,1)} async-done(((bf16[16,32,1024]{2,1,0:T(8,128)(2,1)}), bf16[16,32,1024]{2,1,0:T(8,128)(2,1)}, u32[]{:S(2)}, u32[]{:S(2)}) %all-to-all-start.5) | async-done | bytes 1048608 | tf_op jit(solution)/shard_map/all_to_all | solution.py:26
  169.7 4.0 %convolution_convert_fusion = bf16[512,896]{1,0:T(8,128)(2,1)} fusion(bf16[512,1024]{1,0:T(8,128)(2,1)} %bitcast.27, bf16[896,1024]{1,0:T(8,128)(2,1)} %broadcast_select_fusion.6), kind=kOutput, calls=%fused_computation.79 | convolution fusion | flops 939982848 | bytes 3801088 | tf_op jit(solution)/shard_map/dot_general | solution.py:14
  173.7 4.4 %all-to-all-start.6 = ((bf16[8,64,896]{2,1,0:T(8,128)(2,1)}), bf16[8,64,896]{2,1,0:T(8,128)(2,1)}, u32[]{:S(2)}, u32[]{:S(2)}) async-start(bf16[8,64,896]{2,1,0:T(8,128)(2,1)} %bitcast.161), calls=%async_computation.6 | async-start | bytes 1835008 | tf_op jit(solution)/shard_map/all_to_all | solution.py:26
  179.1 3.7 %broadcast_select_fusion = (bf16[2,512,896]{2,1,0:T(8,128)(2,1)}, bf16[2,512,896]{2,1,0:T(8,128)(2,1)}) fusion(bf16[2,512,896]{2,1,0:T(8,128)(2,1)} %bitcast.155, bf16[2,512,896]{2,1,0:T(8,128)(2,1)S(1)} %bitcast.154, pred[]{:T(512)S(6)} %eq.3), kind=kLoop, calls=%fused_computation.70 | loop fusion | flops 1835008 | bytes 7340033 | tf_op jit(solution)/shard_map/jit(_where)/select_n | solution.py:119
  182.8 4.6 %collective-permute-start.6 = (bf16[2,512,896]{2,1,0:T(8,128)(2,1)}, bf16[2,512,896]{2,1,0:T(8,128)(2,1)S(1)}, u32[]{:S(2)}, u32[]{:S(2)}) collective-permute-start(bf16[2,512,896]{2,1,0:T(8,128)(2,1)} %get-tuple-element.70), channel_id=1, source_target_pairs={{0,128},{128,0},{1,129},{129,1},{2,130},{130,2},{3,131},{131,3},{4... | collective-permute-start | bytes 5505032 | tf_op jit(solution)/shard_map/ppermute | solution.py:18
  187.4 13.3 %all-to-all-done.6 = bf16[8,64,896]{2,1,0:T(8,128)(2,1)} async-done(((bf16[8,64,896]{2,1,0:T(8,128)(2,1)}), bf16[8,64,896]{2,1,0:T(8,128)(2,1)}, u32[]{:S(2)}, u32[]{:S(2)}) %all-to-all-start.6) | async-done | bytes 917536 | tf_op jit(solution)/shard_map/all_to_all | solution.py:26
  200.7 1.3 reduce_sum.113
  202.0 1.1 broadcast_in_dim.24
  203.1 4.2 %all-to-all-start.7 = ((bf16[8,64,896]{2,1,0:T(8,128)(2,1)}), bf16[8,64,896]{2,1,0:T(8,128)(2,1)}, u32[]{:S(2)}, u32[]{:S(2)}) async-start(bf16[8,64,896]{2,1,0:T(8,128)(2,1)} %broadcast_in_dim.24), calls=%async_computation.7 | async-start | bytes 1835008 | tf_op jit(solution)/shard_map/all_to_all | solution.py:26
  207.4 1.5 broadcast_select_fusion.9
  208.9 4.4 %collective-permute-start.7 = (bf16[512,1024]{1,0:T(8,128)(2,1)S(1)}, bf16[512,1024]{1,0:T(8,128)(2,1)S(1)}, u32[]{:S(2)}, u32[]{:S(2)}) collective-permute-start(bf16[512,1024]{1,0:T(8,128)(2,1)S(1)} %get-tuple-element.78), channel_id=1, source_target_pairs={{0,128},{128,0},{1,129},{129,1},{2,130},{130,2},{3,131},{131,3},{4... | collective-permute-start | bytes 3145736 | tf_op jit(solution)/shard_map/ppermute | solution.py:18
  213.4 1.3 collective-permute-start.8
  215.8 3.4 %fusion.52 = bf16[896,1024]{1,0:T(8,128)(2,1)} fusion(bf16[512,1024]{1,0:T(8,128)(2,1)S(1)} %collective-permute-done.7, bf16[512,1024]{1,0:T(8,128)(2,1)S(1)} %get-tuple-element.77, bf16[512,896]{1,0:T(8,128)(2,1)S(1)} %fusion.14, bf16[512,896]{1,0:T(8,128)(2,1)S(1)} %fusion.47), kind=kOutput, calls=%fused_computation.78 | convolution fusion | flops 1887830016 | bytes 5767168 | tf_op jit(solution)/shard_map/dot_general | solution.py:14
  219.2 10.9 %all-to-all-done.7 = bf16[8,64,896]{2,1,0:T(8,128)(2,1)} async-done(((bf16[8,64,896]{2,1,0:T(8,128)(2,1)}), bf16[8,64,896]{2,1,0:T(8,128)(2,1)}, u32[]{:S(2)}, u32[]{:S(2)}) %all-to-all-start.7) | async-done | bytes 917536 | tf_op jit(solution)/shard_map/all_to_all | solution.py:26
  230.1 7.1 %collective-permute-start.15 = (bf16[512,896]{1,0:T(8,128)(2,1)}, bf16[512,896]{1,0:T(8,128)(2,1)}, u32[]{:S(2)}, u32[]{:S(2)}) collective-permute-start(bf16[512,896]{1,0:T(8,128)(2,1)} %bitcast.30), channel_id=1, source_target_pairs={{128,0},{129,1},{130,2},{131,3},{132,4},{133,5},{134,6},{135,7},{1... | collective-permute-start | bytes 2752520 | tf_op jit(solution)/shard_map/ppermute | solution.py:124
  237.2 3.1 %fusion.9 = (bf16[512,896]{1,0:T(8,128)(2,1)S(1)}, bf16[512,896]{1,0:T(8,128)(2,1)S(1)}) fusion(bf16[512,896]{1,0:T(8,128)(2,1)} %bitcast.30, bf16[2,1,512,896]{3,2,1,0:T(8,128)(2,1)} %bitcast.156, bf16[2,1,512,896]{3,2,0,1:T(8,128)(2,1)} %all-gather.6.cloned.1.call-done), kind=kLoop, calls=%fused_computation.29 | loop fusion | flops 7340032 | bytes 4587520 | tf_op jit(solution)/shard_map/convert_element_type | solution.py:38
  240.3 1.3 fusion.84
  241.6 0.8 copy-done.12
  242.4 2.3 add_convert_fusion
  244.7 4.3 %all-to-all-start.8 = ((bf16[16,32,1024]{2,1,0:T(8,128)(2,1)}), bf16[16,32,1024]{2,1,0:T(8,128)(2,1)S(1)}, u32[]{:S(2)}, u32[]{:S(2)}) async-start(bf16[16,32,1024]{2,1,0:T(8,128)(2,1)} %bitcast.160), calls=%async_computation.8 | async-start | bytes 2097152 | tf_op jit(solution)/shard_map/all_to_all | solution.py:26
  249.1 1.4 broadcast_select_fusion.12
  250.9 1.1 copy-done.15
  252.1 1.0 fusion.35
  253.7 3.6 %convert_bitcast_fusion.1 = bf16[1,1024,896]{2,1,0:T(8,128)(2,1)} fusion(bf16[1024,1024]{1,0:T(8,128)(2,1)S(1)} %bitcast.182, bf16[512,896]{1,0:T(8,128)(2,1)S(1)} %get-tuple-element.72, bf16[512,896]{1,0:T(8,128)(2,1)S(1)} %broadcast_select_fusion.12), kind=kOutput, calls=%fused_computation.68 | convolution fusion | flops 1883635712 | bytes 5767168 | tf_op jit(solution)/shard_map/dot_general | solution.py:14
  257.4 3.6 %convert_bitcast_fusion = bf16[1,1024,896]{2,1,0:T(8,128)(2,1)} fusion(bf16[1024,1024]{1,0:T(8,128)(2,1)S(1)} %bitcast.183, bf16[512,896]{1,0:T(8,128)(2,1)S(1)} %get-tuple-element.71, bf16[512,896]{1,0:T(8,128)(2,1)S(1)} %broadcast_select_fusion.10), kind=kOutput, calls=%fused_computation.67 | convolution fusion | flops 1883635712 | bytes 5767168 | tf_op jit(solution)/shard_map/dot_general | solution.py:14
  261.0 5.3 %all-to-all-done.8 = bf16[16,32,1024]{2,1,0:T(8,128)(2,1)S(1)} async-done(((bf16[16,32,1024]{2,1,0:T(8,128)(2,1)}), bf16[16,32,1024]{2,1,0:T(8,128)(2,1)S(1)}, u32[]{:S(2)}, u32[]{:S(2)}) %all-to-all-start.8) | async-done | bytes 1048608 | tf_op jit(solution)/shard_map/all_to_all | solution.py:26
  266.8 1.5 collective-permute-start.10
  268.2 2.1 collective-permute-start.9
  272.4 3.5 %all-to-all-start.9 = ((f32[16,2,1024]{2,1,0:T(2,128)}), f32[16,2,1024]{2,1,0:T(2,128)S(1)}, u32[]{:S(2)}, u32[]{:S(2)}) async-start(f32[16,2,1024]{2,1,0:T(2,128)} %broadcast_in_dim.25), calls=%async_computation.9 | async-start | bytes 262144 | tf_op jit(solution)/shard_map/all_to_all | solution.py:26
  275.9 1.6 collective-permute-done.12
  277.7 2.3 collective-permute-start.13
  280.0 2.7 all-to-all-done.9
  282.8 3.5 %collective-permute-start.14 = (f32[1024]{0:T(1024)S(1)}, f32[1024]{0:T(1024)S(1)}, u32[]{:S(2)}, u32[]{:S(2)}) collective-permute-start(f32[1024]{0:T(1024)S(1)} %bitcast.179), channel_id=1, source_target_pairs={{0,128},{128,0},{1,129},{129,1},{2,130},{130,2},{3,131},{131,3},{4... | collective-permute-start | bytes 12296 | tf_op jit(solution)/shard_map/ppermute | solution.py:18
  (97 shorter events, 10.9 us)
Async XLA Ops:
  7.2 8.1 %copy-start.17 = (bf16[64,1024]{1,0:T(8,128)(2,1)S(1)}, bf16[64,1024]{1,0:T(8,128)(2,1)}, u32[]{:S(2)}) copy-start(bf16[64,1024]{1,0:T(8,128)(2,1)} %param.15) | copy-start | bytes 393220
  7.2 69.0 %all-gather.4.cloned.1.call-start = ((), (), s32[]{:S(2)}) async-start(), calls=%async_computation.10 | async-start | bytes 2064384 | tf_op jit(solution)/shard_map/all_gather | solution.py:71
  8.3 4.4 %collective-permute-start.1 = (bf16[2,2,32,896]{3,2,1,0:T(8,128)(2,1)S(1)}, bf16[2,2,32,896]{3,2,1,0:T(8,128)(2,1)S(1)}, u32[]{:S(2)}, u32[]{:S(2)}) collective-permute-start(bf16[2,2,32,896]{3,2,1,0:T(8,128)(2,1)S(1)} %fusion.61), channel_id=1, source_target_pairs={{0,128},{128,0},{1,129},{129,1},{2,130},{130,2},{3,131},{131,3},{4... | collective-permute-start | bytes 688136 | tf_op jit(solution)/shard_map/ppermute | solution.py:18
  12.8 8.6 %collective-permute-start.2 = (bf16[896,1024]{1,0:T(8,128)(2,1)}, bf16[896,1024]{1,0:T(8,128)(2,1)}, u32[]{:S(2)}, u32[]{:S(2)}) collective-permute-start(bf16[896,1024]{1,0:T(8,128)(2,1)} %bitcast.147), channel_id=1, source_target_pairs={{0,128},{128,0},{1,129},{129,1},{2,130},{130,2},{3,131},{131,3},{4... | collective-permute-start | bytes 5505032 | tf_op jit(solution)/shard_map/ppermute | solution.py:18
  15.2 6.2 %copy-start = (bf16[1,896,1024]{2,1,0:T(8,128)(2,1)S(1)}, bf16[1,896,1024]{2,1,0:T(8,128)(2,1)}, u32[]{:S(2)}) copy-start(bf16[1,896,1024]{2,1,0:T(8,128)(2,1)} %param.14) | copy-start | bytes 5505028
  16.4 21.8 %all-to-all-start = ((bf16[16,32,1024]{2,1,0:T(8,128)(2,1)}), bf16[16,32,1024]{2,1,0:T(8,128)(2,1)S(1)}, u32[]{:S(2)}, u32[]{:S(2)}) async-start(bf16[16,32,1024]{2,1,0:T(8,128)(2,1)} %broadcast_in_dim.20), calls=%async_computation | async-start | bytes 2097152 | tf_op jit(solution)/shard_map/all_to_all | solution.py:26
  41.9 33.0 %all-to-all-start.1 = ((bf16[8,64,896]{2,1,0:T(8,128)(2,1)}), bf16[8,64,896]{2,1,0:T(8,128)(2,1)}, u32[]{:S(2)}, u32[]{:S(2)}) async-start(bf16[8,64,896]{2,1,0:T(8,128)(2,1)} %bitcast.162), calls=%async_computation.1 | async-start | bytes 1835008 | tf_op jit(solution)/shard_map/all_to_all | solution.py:26
  50.0 31.5 %collective-permute-start.5 = (bf16[1024,896]{1,0:T(8,128)(2,1)}, bf16[1024,896]{1,0:T(8,128)(2,1)}, u32[]{:S(2)}, u32[]{:S(2)}) collective-permute-start(bf16[1024,896]{1,0:T(8,128)(2,1)} %bitcast.149), channel_id=1, source_target_pairs={{0,128},{128,0},{1,129},{129,1},{2,130},{130,2},{3,131},{131,3},{4... | collective-permute-start | bytes 5505032 | tf_op jit(solution)/shard_map/ppermute | solution.py:18
  52.2 32.4 %collective-permute-start.4 = (bf16[1024,896]{1,0:T(8,128)(2,1)}, bf16[1024,896]{1,0:T(8,128)(2,1)}, u32[]{:S(2)}, u32[]{:S(2)}) collective-permute-start(bf16[1024,896]{1,0:T(8,128)(2,1)} %bitcast.151), channel_id=1, source_target_pairs={{0,128},{128,0},{1,129},{129,1},{2,130},{130,2},{3,131},{131,3},{4... | collective-permute-start | bytes 5505032 | tf_op jit(solution)/shard_map/ppermute | solution.py:18
  77.3 30.6 %all-to-all-start.2 = ((bf16[8,64,896]{2,1,0:T(8,128)(2,1)}), bf16[8,64,896]{2,1,0:T(8,128)(2,1)}, u32[]{:S(2)}, u32[]{:S(2)}) async-start(bf16[8,64,896]{2,1,0:T(8,128)(2,1)} %broadcast_in_dim.21), calls=%async_computation.2 | async-start | bytes 1835008 | tf_op jit(solution)/shard_map/all_to_all | solution.py:26
  81.5 3.1 %copy-start.1 = (bf16[1,1024,896]{2,1,0:T(8,128)(2,1)S(1)}, bf16[1,1024,896]{2,1,0:T(8,128)(2,1)}, u32[]{:S(2)}) copy-start(bf16[1,1024,896]{2,1,0:T(8,128)(2,1)} %param.12) | copy-start | bytes 5505028
  107.9 2.9 copy-start.10
  110.7 1.3 copy-start.4
  110.7 1.3 copy-start.6
  110.7 2.2 copy-start.11
  115.1 6.2 %copy-start.18 = (f32[1,1024]{1,0:T(1,128)S(1)}, f32[1,1024]{1,0:T(1,128)}, u32[]{:S(2)}) copy-start(f32[1,1024]{1,0:T(1,128)} %param.9) | copy-start | bytes 12292
  115.1 7.1 %copy-start.16 = (bf16[1,64,1024]{2,1,0:T(8,128)(2,1)S(1)}, bf16[1,64,1024]{2,1,0:T(8,128)(2,1)}, u32[]{:S(2)}) copy-start(bf16[1,64,1024]{2,1,0:T(8,128)(2,1)} %param.8) | copy-start | bytes 393220
  115.1 22.4 %all-to-all-start.3 = ((bf16[16,32,1024]{2,1,0:T(8,128)(2,1)}), bf16[16,32,1024]{2,1,0:T(8,128)(2,1)}, u32[]{:S(2)}, u32[]{:S(2)}) async-start(bf16[16,32,1024]{2,1,0:T(8,128)(2,1)} %bitcast.159), calls=%async_computation.3 | async-start | bytes 2097152 | tf_op jit(solution)/shard_map/all_to_all | solution.py:26
  121.3 52.4 %all-gather.6.cloned.1.call-start = ((), (), s32[]{:S(2)}) async-start(), calls=%async_computation.11 | async-start | bytes 2064384 | tf_op jit(solution)/shard_map/all_gather | solution.py:71
  121.4 1.7 collective-permute-start.3
  122.2 16.8 %collective-permute-start = (bf16[32,1024]{1,0:T(8,128)(2,1)S(1)}, bf16[32,1024]{1,0:T(8,128)(2,1)S(1)}, u32[]{:S(2)}, u32[]{:S(2)}) collective-permute-start(bf16[32,1024]{1,0:T(8,128)(2,1)S(1)} %select_bitcast_fusion.1), channel_id=1, source_target_pairs={{0,128},{128,0},{1,129},{129,1},{2,130},{130,2},{3,131},{131,3},{4... | collective-permute-start | bytes 196616 | tf_op jit(solution)/shard_map/ppermute | solution.py:18
  151.2 18.5 %all-to-all-start.5 = ((bf16[16,32,1024]{2,1,0:T(8,128)(2,1)}), bf16[16,32,1024]{2,1,0:T(8,128)(2,1)}, u32[]{:S(2)}, u32[]{:S(2)}) async-start(bf16[16,32,1024]{2,1,0:T(8,128)(2,1)} %broadcast_in_dim.23), calls=%async_computation.5 | async-start | bytes 2097152 | tf_op jit(solution)/shard_map/all_to_all | solution.py:26
  173.7 5.3 %copy-start.3 = (bf16[2,1,512,896]{3,2,0,1:T(8,128)(2,1)S(1)}, bf16[2,1,512,896]{3,2,0,1:T(8,128)(2,1)}, u32[]{:S(2)}) copy-start(bf16[2,1,512,896]{3,2,0,1:T(8,128)(2,1)} %all-gather.4.cloned.1.call-done) | copy-start | bytes 5505028
  173.7 27.0 %all-to-all-start.6 = ((bf16[8,64,896]{2,1,0:T(8,128)(2,1)}), bf16[8,64,896]{2,1,0:T(8,128)(2,1)}, u32[]{:S(2)}, u32[]{:S(2)}) async-start(bf16[8,64,896]{2,1,0:T(8,128)(2,1)} %bitcast.161), calls=%async_computation.6 | async-start | bytes 1835008 | tf_op jit(solution)/shard_map/all_to_all | solution.py:26
  178.1 66.6 %all-gather.8.cloned.1.call-start = ((), (), s32[]{:S(2)}) async-start(), calls=%async_computation.12 | async-start | bytes 2228224 | tf_op jit(solution)/shard_map/all_gather | solution.py:158
  182.8 32.5 %collective-permute-start.6 = (bf16[2,512,896]{2,1,0:T(8,128)(2,1)}, bf16[2,512,896]{2,1,0:T(8,128)(2,1)S(1)}, u32[]{:S(2)}, u32[]{:S(2)}) collective-permute-start(bf16[2,512,896]{2,1,0:T(8,128)(2,1)} %get-tuple-element.70), channel_id=1, source_target_pairs={{0,128},{128,0},{1,129},{129,1},{2,130},{130,2},{3,131},{131,3},{4... | collective-permute-start | bytes 5505032 | tf_op jit(solution)/shard_map/ppermute | solution.py:18
  203.1 26.9 %all-to-all-start.7 = ((bf16[8,64,896]{2,1,0:T(8,128)(2,1)}), bf16[8,64,896]{2,1,0:T(8,128)(2,1)}, u32[]{:S(2)}, u32[]{:S(2)}) async-start(bf16[8,64,896]{2,1,0:T(8,128)(2,1)} %broadcast_in_dim.24), calls=%async_computation.7 | async-start | bytes 1835008 | tf_op jit(solution)/shard_map/all_to_all | solution.py:26
  207.4 7.3 %copy-start.2 = (bf16[2,512,896]{2,1,0:T(8,128)(2,1)S(1)}, bf16[2,512,896]{2,1,0:T(8,128)(2,1)}, u32[]{:S(2)}) copy-start(bf16[2,512,896]{2,1,0:T(8,128)(2,1)} %get-tuple-element.69) | copy-start | bytes 5505028
  208.9 6.9 %collective-permute-start.7 = (bf16[512,1024]{1,0:T(8,128)(2,1)S(1)}, bf16[512,1024]{1,0:T(8,128)(2,1)S(1)}, u32[]{:S(2)}, u32[]{:S(2)}) collective-permute-start(bf16[512,1024]{1,0:T(8,128)(2,1)S(1)} %get-tuple-element.78), channel_id=1, source_target_pairs={{0,128},{128,0},{1,129},{129,1},{2,130},{130,2},{3,131},{131,3},{4... | collective-permute-start | bytes 3145736 | tf_op jit(solution)/shard_map/ppermute | solution.py:18
  213.4 23.8 %collective-permute-start.8 = (bf16[512,896]{1,0:T(8,128)(2,1)}, bf16[512,896]{1,0:T(8,128)(2,1)S(1)}, u32[]{:S(2)}, u32[]{:S(2)}) collective-permute-start(bf16[512,896]{1,0:T(8,128)(2,1)} %bitcast.14), channel_id=1, source_target_pairs={{0,128},{1,129},{2,130},{3,131},{4,132},{5,133},{6,134},{7,135},{8... | collective-permute-start | bytes 2752520 | tf_op jit(solution)/shard_map/ppermute | solution.py:124
  230.1 20.9 %collective-permute-start.15 = (bf16[512,896]{1,0:T(8,128)(2,1)}, bf16[512,896]{1,0:T(8,128)(2,1)}, u32[]{:S(2)}, u32[]{:S(2)}) collective-permute-start(bf16[512,896]{1,0:T(8,128)(2,1)} %bitcast.30), channel_id=1, source_target_pairs={{128,0},{129,1},{130,2},{131,3},{132,4},{133,5},{134,6},{135,7},{1... | collective-permute-start | bytes 2752520 | tf_op jit(solution)/shard_map/ppermute | solution.py:124
  237.2 3.1 %copy-start.14 = (bf16[512,896]{1,0:T(8,128)(2,1)}, bf16[512,896]{1,0:T(8,128)(2,1)S(1)}, u32[]{:S(2)}) copy-start(bf16[512,896]{1,0:T(8,128)(2,1)S(1)} %collective-permute-done.8) | copy-start | bytes 2752516
  237.2 3.1 %copy-start.13 = (bf16[1024,896]{1,0:T(8,128)(2,1)S(1)}, bf16[1024,896]{1,0:T(8,128)(2,1)}, u32[]{:S(2)}) copy-start(bf16[1024,896]{1,0:T(8,128)(2,1)} %get-tuple-element.91) | copy-start | bytes 5505028
  240.3 1.3 copy-start.7
  240.3 1.3 copy-start.9
  240.3 2.2 copy-start.12
  244.7 21.6 %all-to-all-start.8 = ((bf16[16,32,1024]{2,1,0:T(8,128)(2,1)}), bf16[16,32,1024]{2,1,0:T(8,128)(2,1)S(1)}, u32[]{:S(2)}, u32[]{:S(2)}) async-start(bf16[16,32,1024]{2,1,0:T(8,128)(2,1)} %bitcast.160), calls=%async_computation.8 | async-start | bytes 2097152 | tf_op jit(solution)/shard_map/all_to_all | solution.py:26
  249.1 1.5 copy-start.5
  249.1 1.7 copy-start.8
  250.8 1.2 copy-start.15
  252.1 1.6 copy-start.19
  266.7 4.3 %collective-permute-start.11 = (f32[32]{0:T(128)S(1)}, f32[32]{0:T(128)S(1)}, u32[]{:S(2)}, u32[]{:S(2)}) collective-permute-start(f32[32]{0:T(128)S(1)} %get-tuple-element.62), channel_id=1, source_target_pairs={{0,48},{16,32},{32,16},{48,0},{64,112},{80,96},{96,80},{112,64},{1... | collective-permute-start | bytes 392 | tf_op jit(solution)/shard_map/ppermute | solution.py:178
  266.8 4.2 %collective-permute-start.10 = (f32[32]{0:T(128)S(1)}, f32[32]{0:T(128)S(1)}, u32[]{:S(2)}, u32[]{:S(2)}) collective-permute-start(f32[32]{0:T(128)S(1)} %get-tuple-element.62), channel_id=1, source_target_pairs={{0,32},{16,48},{32,0},{48,16},{64,96},{80,112},{96,64},{112,80},{1... | collective-permute-start | bytes 392 | tf_op jit(solution)/shard_map/ppermute | solution.py:178
  268.2 3.0 %collective-permute-start.9 = (f32[32]{0:T(128)S(1)}, f32[32]{0:T(128)S(1)}, u32[]{:S(2)}, u32[]{:S(2)}) collective-permute-start(f32[32]{0:T(128)S(1)} %get-tuple-element.62), channel_id=1, source_target_pairs={{0,16},{16,0},{32,48},{48,32},{64,80},{80,64},{96,112},{112,96},{1... | collective-permute-start | bytes 392 | tf_op jit(solution)/shard_map/ppermute | solution.py:178
  271.2 6.3 %collective-permute-start.12 = (f32[32]{0:T(128)S(1)}, f32[32]{0:T(128)S(1)}, u32[]{:S(2)}, u32[]{:S(2)}) collective-permute-start(f32[32]{0:T(128)S(1)} %add_add_fusion), channel_id=1, source_target_pairs={{0,64},{16,80},{32,96},{48,112},{64,0},{80,16},{96,32},{112,48},{1... | collective-permute-start | bytes 392 | tf_op jit(solution)/shard_map/ppermute | solution.py:180
  272.4 10.3 %all-to-all-start.9 = ((f32[16,2,1024]{2,1,0:T(2,128)}), f32[16,2,1024]{2,1,0:T(2,128)S(1)}, u32[]{:S(2)}, u32[]{:S(2)}) async-start(f32[16,2,1024]{2,1,0:T(2,128)} %broadcast_in_dim.25), calls=%async_computation.9 | async-start | bytes 262144 | tf_op jit(solution)/shard_map/all_to_all | solution.py:26
  277.7 8.6 %collective-permute-start.13 = (bf16[32,1024]{1,0:T(8,128)(2,1)S(1)}, bf16[32,1024]{1,0:T(8,128)(2,1)S(1)}, u32[]{:S(2)}, u32[]{:S(2)}) collective-permute-start(bf16[32,1024]{1,0:T(8,128)(2,1)S(1)} %get-tuple-element.82), channel_id=1, source_target_pairs={{0,128},{128,0},{1,129},{129,1},{2,130},{130,2},{3,131},{131,3},{4... | collective-permute-start | bytes 196616 | tf_op jit(solution)/shard_map/ppermute | solution.py:18
  282.8 4.3 %collective-permute-start.14 = (f32[1024]{0:T(1024)S(1)}, f32[1024]{0:T(1024)S(1)}, u32[]{:S(2)}, u32[]{:S(2)}) collective-permute-start(f32[1024]{0:T(1024)S(1)} %bitcast.179), channel_id=1, source_target_pairs={{0,128},{128,0},{1,129},{129,1},{2,130},{130,2},{3,131},{131,3},{4... | collective-permute-start | bytes 12296 | tf_op jit(solution)/shard_map/ppermute | solution.py:18
Sparse Core Ops, SparseCore 0:
  15.3 37.7 all-gather.3
  123.9 33.5 all-gather.5
  182.0 50.7 all-gather.7
